TPU v7x, 32 devices: a whole 2x2x4 slice. The times are simulated.
32 devices in a mesh: section: 2 (over core), dp: 4 (over z), seq: 4 (over y, x).
Axes of the slice: x: 2, y: 2, z: 4, core: 2. Of those that a mesh axis runs over, the one named last changes fastest.
Arguments:
- block_inputs: bfloat16 [2, 16, 768, 800], P('section', 'dp', 'seq'), may hold values from -6 to 6
- cotangent: bfloat16 [16, 768, 800], P('dp', 'seq'), may hold values from -6 to 6
- segment_ids: int32 [16, 768], P('dp', 'seq'), may hold values from 0 to 7, as said below
- in_gain: float32 [2, 800], P('section'), may hold values from 0.5 to 1.5
- in_shift: float32 [2, 800], P('section'), may hold values from -3 to 3
- down_weight: bfloat16 [2, 800, 400], P('section'), may hold values from -0.21875 to 0.21875
- down_bias: float32 [2, 400], P('section'), may hold values from -3 to 3
- mid_gain: float32 [2, 400], P('section'), may hold values from 0.5 to 1.5
- mid_shift: float32 [2, 400], P('section'), may hold values from -3 to 3
- enc_kernel: bfloat16 [5, 400, 400], replicated, may hold values from -0.125 to 0.125
- dec_kernel: bfloat16 [3, 400, 400], replicated, may hold values from -0.1875 to 0.1875
- conv_bias: float32 [2, 400], P('section'), may hold values from -3 to 3
- out_gain: float32 [2, 400], P('section'), may hold values from 0.5 to 1.5
- out_shift: float32 [2, 400], P('section'), may hold values from -3 to 3
- up_weight: bfloat16 [2, 400, 800], P('section'), may hold values from -0.3125 to 0.3125
- up_bias: float32 [2, 800], P('section'), may hold values from -3 to 3
Outputs:
- block_outputs: bfloat16 [2, 16, 768, 800], P('section', 'dp', 'seq')
- input_grads: bfloat16 [2, 16, 768, 800], P('section', 'dp', 'seq')
- in_gain_grad: float32 [2, 800], P('section')
- in_shift_grad: float32 [2, 800], P('section')
- down_weight_grad: float32 [2, 800, 400], P('section')
- down_bias_grad: float32 [2, 400], P('section')
- mid_gain_grad: float32 [2, 400], P('section')
- mid_shift_grad: float32 [2, 400], P('section')
- enc_kernel_grad: float32 [5, 400, 400], P(None, None, 'section')
- dec_kernel_grad: float32 [3, 400, 400], P(None, None, 'section')
- conv_bias_grad: float32 [2, 400], P('section')
- out_gain_grad: float32 [2, 400], P('section')
- out_shift_grad: float32 [2, 400], P('section')
- up_weight_grad: float32 [2, 400, 800], P('section')
- up_bias_grad: float32 [2, 800], P('section')
Inputs may be any that keep to these rules, and one draw needn't show every extreme that they name: `segment_ids`: along each row the segment numbers never fall and start at 0; equal numbers mark one sentence pair.
All inputs are finite; a program needn't handle non-finite values.
Results may differ from a plain program's by a relative error of at most 0.0085.
Values may be sent and summed in bfloat16 or wider, within the bound.
A program may use at most 192 MiB of HBM per device.

v0:
```python
import jax
import jax.numpy as jnp
from jax import lax
from jax.sharding import PartitionSpec as P

DILATION = 16
MICRO = 4


epsilon = 1e-05


def extended_2(array, sides, width):
    for axis, dim in sides:
        devices, length = (lax.axis_size(axis), array.shape[dim])
        up = [(i, (i + 1) % devices) for i in range(devices - 1)]
        down = [(j, i) for i, j in up]
        last = lax.slice_in_dim(array, length - width, length, axis=dim)
        leading = lax.slice_in_dim(array, 0, width, axis=dim)
        before = lax.ppermute(last, axis, up)
        after = lax.ppermute(leading, axis, down)
        array = jnp.concatenate([before, array, after], axis=dim)
    return array


def from_behind(array, axis, by):
    devices = lax.axis_size(axis)
    pairs = [(i, i + by) for i in range(devices) if 0 <= i + by < devices]
    return lax.ppermute(array, axis, pairs)


def normalize(values, gain, shift):
    average = jnp.mean(values, axis=-1, keepdims=True)
    centred = values - average
    variance = jnp.mean(centred * centred, axis=-1, keepdims=True)
    factor = lax.rsqrt(variance + epsilon)
    normed = centred * factor
    return (normed * gain + shift, normed, factor)


def norm_back(upstream, normed, factor, gain):
    scaled = upstream * gain
    first_mean = jnp.mean(scaled, axis=-1, keepdims=True)
    second_mean = jnp.mean(scaled * normed, axis=-1, keepdims=True)
    entry_grad = factor * (scaled - first_mean - normed * second_mean)
    return (entry_grad, jnp.sum(upstream * normed, axis=(0, 1)), jnp.sum(upstream, axis=(0, 1)))


def gelu_back(pre_act, upstream):
    return jax.vjp(jax.nn.gelu, pre_act)[1](upstream)[0]


def windows(extended, tap_masks, length, direction):
    margin = 2 * DILATION
    pieces = []
    for tap in range(5):
        offset = direction * (tap - 2) * DILATION
        piece = lax.slice_in_dim(extended, margin + offset, margin + offset + length, axis=1)
        which = tap if direction > 0 else 4 - tap
        pieces.append(piece * tap_masks[which][..., None])
    return jnp.concatenate(pieces, axis=-1)


def block_forward(block_entry, weights, tap_masks, kernel_rows):
    (
        in_gain,
        in_shift,
        down_weight,
        down_bias,
        mid_gain,
        mid_shift,
        conv_bias,
        out_gain,
        out_shift,
        up_weight,
        up_bias,
    ) = weights
    first_pre, first_normed, first_factor = normalize(block_entry, in_gain, in_shift)
    first_act = jax.nn.gelu(first_pre).astype(jnp.bfloat16)
    hidden = (
        jnp.einsum("rtd,dh->rth", first_act, down_weight, preferred_element_type=jnp.float32)
        + down_bias
    )
    mid_pre, mid_normed, mid_factor = normalize(hidden, mid_gain, mid_shift)
    mid_act = jax.nn.gelu(mid_pre).astype(jnp.bfloat16)
    extended = extended_2(mid_act, (("seq", 1),), 2 * DILATION)
    windowed = windows(extended, tap_masks, mid_act.shape[1], 1)
    conv_out = (
        jnp.einsum("rtk,kh->rth", windowed, kernel_rows, preferred_element_type=jnp.float32)
        + conv_bias
    )
    last_pre, last_normed, last_factor = normalize(conv_out, out_gain, out_shift)
    last_act = jax.nn.gelu(last_pre).astype(jnp.bfloat16)
    result = (
        block_entry
        + jnp.einsum("rth,hd->rtd", last_act, up_weight, preferred_element_type=jnp.float32)
        + up_bias
    )
    return (result, (block_entry, first_act, hidden, windowed, conv_out, last_act))


def block_backward(upstream, stored, weights, tap_masks, kernel_cols):
    block_entry, first_act, hidden, windowed, conv_out, last_act = stored
    (
        in_gain,
        in_shift,
        down_weight,
        down_bias,
        mid_gain,
        mid_shift,
        conv_bias,
        out_gain,
        out_shift,
        up_weight,
        up_bias,
    ) = weights
    first_pre, first_normed, first_factor = normalize(block_entry, in_gain, in_shift)
    mid_pre, mid_normed, mid_factor = normalize(hidden, mid_gain, mid_shift)
    last_pre, last_normed, last_factor = normalize(conv_out, out_gain, out_shift)
    up_rounded = upstream.astype(jnp.bfloat16)
    grad_up_bias = jnp.sum(upstream, axis=(0, 1))
    grad_up_weight = jnp.einsum(
        "rth,rtd->hd", last_act, up_rounded, preferred_element_type=jnp.float32
    )
    last_grad = jnp.einsum("rtd,hd->rth", up_rounded, up_weight, preferred_element_type=jnp.float32)
    conv_grad, grad_out_gain, grad_out_shift = norm_back(
        gelu_back(last_pre, last_grad), last_normed, last_factor, out_gain
    )
    grad_conv_bias = jnp.sum(conv_grad, axis=(0, 1))
    conv_rounded = conv_grad.astype(jnp.bfloat16)
    grad_kernel = jnp.einsum(
        "rtk,rth->kh", windowed, conv_rounded, preferred_element_type=jnp.float32
    )
    grad_ext = extended_2(conv_rounded, (("seq", 1),), 2 * DILATION)
    back_windows = windows(grad_ext, tap_masks, conv_rounded.shape[1], -1)
    mid_grad = jnp.einsum(
        "rtk,kh->rth", back_windows, kernel_cols, preferred_element_type=jnp.float32
    )
    hidden_grad, grad_mid_gain, grad_mid_shift = norm_back(
        gelu_back(mid_pre, mid_grad), mid_normed, mid_factor, mid_gain
    )
    grad_down_bias = jnp.sum(hidden_grad, axis=(0, 1))
    hidden_rounded = hidden_grad.astype(jnp.bfloat16)
    grad_down_weight = jnp.einsum(
        "rtd,rth->dh", first_act, hidden_rounded, preferred_element_type=jnp.float32
    )
    first_grad = jnp.einsum(
        "rth,dh->rtd", hidden_rounded, down_weight, preferred_element_type=jnp.float32
    )
    entry_grad, grad_in_gain, grad_in_shift = norm_back(
        gelu_back(first_pre, first_grad), first_normed, first_factor, in_gain
    )
    grads = (
        grad_in_gain,
        grad_in_shift,
        grad_down_weight,
        grad_down_bias,
        grad_mid_gain,
        grad_mid_shift,
        grad_conv_bias,
        grad_out_gain,
        grad_out_shift,
        grad_up_weight,
        grad_up_bias,
    )
    return (upstream + entry_grad, grads, grad_kernel)


def per_device(
    block_inputs,
    cotangent,
    segment_ids,
    in_gain,
    in_shift,
    down_weight,
    down_bias,
    mid_gain,
    mid_shift,
    enc_kernel,
    dec_kernel,
    conv_bias,
    out_gain,
    out_shift,
    up_weight,
    up_bias,
):
    section_index = lax.axis_index("section")
    encoding = section_index == 0
    row_count = block_inputs.shape[1]
    length = block_inputs.shape[2]
    model_width = block_inputs.shape[3]
    inner_width = enc_kernel.shape[1]
    per_micro = row_count // MICRO
    own_inputs = block_inputs[0].reshape(MICRO, per_micro, length, model_width)
    cot_micro = cotangent.reshape(MICRO, per_micro, length, model_width)
    weights = tuple(
        (
            arr[0]
            for arr in (
                in_gain,
                in_shift,
                down_weight,
                down_bias,
                mid_gain,
                mid_shift,
                conv_bias,
                out_gain,
                out_shift,
                up_weight,
                up_bias,
            )
        )
    )
    padded_dec = jnp.concatenate(
        [dec_kernel, jnp.zeros((2, inner_width, inner_width), dec_kernel.dtype)], axis=0
    )
    kernel = jnp.where(encoding, enc_kernel, padded_dec)
    kernel_rows = kernel.reshape(5 * inner_width, inner_width)
    kernel_cols = jnp.transpose(kernel, (0, 2, 1)).reshape(5 * inner_width, inner_width)
    margin = 2 * DILATION
    seg_plus = segment_ids + 1
    seg_ext = extended_2(seg_plus, (("seq", 1),), margin)
    mask_list = []
    for tap in range(5):
        offset = (tap - 2) * DILATION
        beside_all = lax.slice_in_dim(seg_ext, margin + offset, margin + offset + length, axis=1)
        mask_list.append(beside_all == seg_plus)
    tap_masks = jnp.stack(mask_list).astype(jnp.bfloat16).reshape(5, MICRO, per_micro, length)
    received = jnp.zeros((per_micro, length, model_width), jnp.bfloat16)
    results = []
    kept = []
    for tick_step in range(MICRO + 1):
        slot_index = jnp.clip(tick_step - section_index, 0, MICRO - 1)
        own_rows = lax.dynamic_index_in_dim(own_inputs, slot_index, 0, keepdims=False).astype(
            jnp.float32
        )
        block_entry = jnp.where(encoding, own_rows, received.astype(jnp.float32) + own_rows)
        mask_now = lax.dynamic_index_in_dim(tap_masks, slot_index, 1, keepdims=False)
        result, stored = block_forward(block_entry, weights, mask_now, kernel_rows)
        rounded = result.astype(jnp.bfloat16)
        results.append(rounded)
        kept.append(stored)
        if tick_step < MICRO:
            received = from_behind(rounded, "section", 1)
    result_stack = jnp.stack(results)
    ordered = lax.dynamic_slice_in_dim(result_stack, section_index, MICRO, 0)
    outputs_local = ordered.reshape(1, row_count, length, model_width)
    kept_stack = jax.tree.map(lambda *items: jnp.stack(items), *kept)
    grad_back = jnp.zeros((per_micro, length, model_width), jnp.bfloat16)
    totals = None
    kernel_total = jnp.zeros((5 * inner_width, inner_width), jnp.float32)
    grad_list = []
    for tick_step in range(MICRO + 1):
        raw_index = MICRO - tick_step - section_index
        is_live = ((raw_index >= 0) & (raw_index < MICRO)).astype(jnp.float32)
        slot_index = jnp.clip(raw_index, 0, MICRO - 1)
        stored_slot = slot_index + section_index
        cot_now = lax.dynamic_index_in_dim(cot_micro, slot_index, 0, keepdims=False).astype(
            jnp.float32
        )
        upstream = jnp.where(encoding, grad_back.astype(jnp.float32), cot_now) * is_live
        mask_now = lax.dynamic_index_in_dim(tap_masks, slot_index, 1, keepdims=False)
        stored = jax.tree.map(
            lambda stacked_arr: lax.dynamic_index_in_dim(
                stacked_arr, stored_slot, 0, keepdims=False
            ),
            kept_stack,
        )
        entry_grad, grads, grad_kernel = block_backward(
            upstream, stored, weights, mask_now, kernel_cols
        )
        totals = grads if totals is None else jax.tree.map(jnp.add, totals, grads)
        kernel_total = kernel_total + grad_kernel
        rounded = entry_grad.astype(jnp.bfloat16)
        grad_list.append(rounded)
        if tick_step < MICRO:
            grad_back = from_behind(rounded, "section", -1)
    grad_stack = jnp.stack(grad_list)
    ordered_grads = jnp.flip(
        lax.dynamic_slice_in_dim(grad_stack, 1 - section_index, MICRO, 0), axis=0
    )
    grads_local = ordered_grads.reshape(1, row_count, length, model_width)
    kernel_full = kernel_total.reshape(5, inner_width, inner_width)
    zero_kernel = jnp.zeros_like(kernel_full)
    enc_part = jnp.where(encoding, kernel_full, zero_kernel)
    dec_part = jnp.where(encoding, zero_kernel[:3], kernel_full[:3])
    (
        grad_in_gain,
        grad_in_shift,
        grad_down_weight,
        grad_down_bias,
        grad_mid_gain,
        grad_mid_shift,
        grad_conv_bias,
        grad_out_gain,
        grad_out_shift,
        grad_up_weight,
        grad_up_bias,
    ) = totals
    summed = lax.psum(
        (
            grad_in_gain,
            grad_in_shift,
            grad_down_weight,
            grad_down_bias,
            grad_mid_gain,
            grad_mid_shift,
            grad_conv_bias,
            grad_out_gain,
            grad_out_shift,
            grad_up_weight,
            grad_up_bias,
            enc_part,
            dec_part,
        ),
        ("dp", "seq"),
    )
    enc_final, dec_final = (
        lax.psum_scatter(
            summed[11].astype(jnp.bfloat16), "section", scatter_dimension=2, tiled=True
        ).astype(jnp.float32),
        lax.psum_scatter(
            summed[12].astype(jnp.bfloat16), "section", scatter_dimension=2, tiled=True
        ).astype(jnp.float32),
    )
    return (
        outputs_local,
        grads_local,
        summed[0][None],
        summed[1][None],
        summed[2][None],
        summed[3][None],
        summed[4][None],
        summed[5][None],
        enc_final,
        dec_final,
        summed[6][None],
        summed[7][None],
        summed[8][None],
        summed[9][None],
        summed[10][None],
    )


def solution(mesh):
    return jax.shard_map(
        per_device,
        mesh=mesh,
        in_specs=(
            P("section", "dp", "seq", None),
            P("dp", "seq", None),
            P("dp", "seq"),
            P("section", None),
            P("section", None),
            P("section", None, None),
            P("section", None),
            P("section", None),
            P("section", None),
            P(),
            P(),
            P("section", None),
            P("section", None),
            P("section", None),
            P("section", None, None),
            P("section", None),
        ),
        out_specs=(
            P("section", "dp", "seq", None),
            P("section", "dp", "seq", None),
            P("section", None),
            P("section", None),
            P("section", None, None),
            P("section", None),
            P("section", None),
            P("section", None),
            P(None, None, "section"),
            P(None, None, "section"),
            P("section", None),
            P("section", None),
            P("section", None),
            P("section", None, None),
            P("section", None),
        ),
        check_vma=False,
    )
```

profile of v0, /device:TPU:0, one launch (start us, length us, event | category | flops | bytes accessed | tf_op | source)
XLA Modules:
  0.0 790.8 jit_solution(10790743990047311435)
XLA Ops:
  10.2 5.5 collective-permute-start.1
  26.9 5.5 collective-permute-start
  51.1 5.5 collective-permute-start.5
  72.6 5.5 collective-permute-start.8
  93.9 5.3 collective-permute-start.11
  126.4 5.7 collective-permute-start.14
  153.3 4.8 collective-permute-start.17
  160.9 4.2 collective-permute-done.16
  179.2 3.6 fusion.25
  187.1 4.8 collective-permute-start.20
  194.0 4.0 collective-permute-done.19
  201.5 3.5 multiply_reduce_fusion.27
  213.6 3.6 fusion.23
  226.4 4.0 collective-permute-done.22
  233.8 3.5 multiply_reduce_fusion.26
  258.3 4.0 collective-permute-done.25
  288.8 4.1 broadcast_select_fusion
  296.9 4.9 copy.37
  317.9 279.3 %all-reduce.7 = (f32[1,800]{1,0:T(1,128)}, f32[1,800]{1,0:T(1,128)}, f32[1,400]{1,0:T(1,128)}, f32[1,400]{1,0:T(1,128)}, f32[1,400]{1,0:T(1,128)}, /*index=5*/bf...) all-reduce(f32[1,800]{1,0:T(1,128)S(1)} %broadcast_in_dim.24, ...), channel_id=1, replica_groups=mesh['section'=2,'dp'=4,'seq'=4] {'dp','seq'}, use_global_device_ids=true, to_apply=%region_95.96 | all-reduce | flops 1284800 | bytes 7718400 | tf_op jit(solution)/shard_map/psum | solution.py:300
  597.2 4.0 copy.41
  601.2 4.2 reshape.2792
  610.7 5.1 copy.39
  615.8 5.9 reshape.2790
  655.3 123.8 %all-reduce.6.cloned.1.call-done = (f32[1,800,400]{1,2,0:T(8,128)}, f32[1,400,800]{2,1,0:T(8,128)}) async-done(((f32[1,800,400]{1,2,0:T(8,128)}, f32[1,400,800]{2,1,0:T(8,128)}), (f32[1,800,400]{1,2,0:T(8,128)}, f32[1,400,800]{2,1,0:T(8,128)})) %all-reduce.6.cloned.1.call-update) | async-done | bytes 2560016 | tf_op jit(solution)/shard_map/psum | solution.py:300
  (866 shorter events, 267.3 us)
Async XLA Ops:
  8.0 636.7 %reduce-scatter.9.cloned.1.call-start = ((), (), s32[]{:S(2)}) async-start(), calls=%async_computation.3 | async-start | bytes 1536000
  8.9 14.8 %collective-permute-start.2 = (s32[4,32]{1,0:T(4,128)S(1)}, s32[4,32]{1,0:T(4,128)S(1)}, u32[]{:S(2)}, u32[]{:S(2)}) collective-permute-start(s32[4,32]{1,0:T(4,128)S(1)} %get-tuple-element.269), channel_id=1, source_target_pairs={{1,0},{2,1},{3,2},{5,4},{6,5},{7,6},{9,8},{10,9},{11,10},{13,12},{... | collective-permute-start | bytes 1544 | tf_op jit(solution)/shard_map/ppermute | solution.py:21
  10.2 13.3 %collective-permute-start.1 = (s32[4,32]{1,0:T(4,128)S(1)}, s32[4,32]{1,0:T(4,128)S(1)}, u32[]{:S(2)}, u32[]{:S(2)}) collective-permute-start(s32[4,32]{1,0:T(4,128)S(1)} %get-tuple-element.270), channel_id=1, source_target_pairs={{0,1},{1,2},{2,3},{4,5},{5,6},{6,7},{8,9},{9,10},{10,11},{12,13},{... | collective-permute-start | bytes 1544 | tf_op jit(solution)/shard_map/ppermute | solution.py:20
  25.6 12.0 %collective-permute-start.3 = (bf16[1,32,400]{2,1,0:T(8,128)(2,1)S(1)}, bf16[1,32,400]{2,1,0:T(8,128)(2,1)S(1)}, u32[]{:S(2)}, u32[]{:S(2)}) collective-permute-start(bf16[1,32,400]{2,1,0:T(8,128)(2,1)S(1)} %get-tuple-element.266), channel_id=1, source_target_pairs={{1,0},{2,1},{3,2},{5,4},{6,5},{7,6},{9,8},{10,9},{11,10},{13,12},{... | collective-permute-start | bytes 76808 | tf_op jit(solution)/shard_map/ppermute | solution.py:21
  26.9 10.7 %collective-permute-start = (bf16[1,32,400]{2,1,0:T(8,128)(2,1)S(1)}, bf16[1,32,400]{2,1,0:T(8,128)(2,1)S(1)}, u32[]{:S(2)}, u32[]{:S(2)}) collective-permute-start(bf16[1,32,400]{2,1,0:T(8,128)(2,1)S(1)} %get-tuple-element.267), channel_id=1, source_target_pairs={{0,1},{1,2},{2,3},{4,5},{5,6},{6,7},{8,9},{9,10},{10,11},{12,13},{... | collective-permute-start | bytes 76808 | tf_op jit(solution)/shard_map/ppermute | solution.py:20
  49.8 8.9 %collective-permute-start.6 = (bf16[1,32,400]{2,1,0:T(8,128)(2,1)S(1)}, bf16[1,32,400]{2,1,0:T(8,128)(2,1)S(1)}, u32[]{:S(2)}, u32[]{:S(2)}) collective-permute-start(bf16[1,32,400]{2,1,0:T(8,128)(2,1)S(1)} %get-tuple-element.262), channel_id=1, source_target_pairs={{1,0},{2,1},{3,2},{5,4},{6,5},{7,6},{9,8},{10,9},{11,10},{13,12},{... | collective-permute-start | bytes 76808 | tf_op jit(solution)/shard_map/ppermute | solution.py:21
  51.1 7.6 collective-permute-start.5
  71.3 8.9 %collective-permute-start.9 = (bf16[1,32,400]{2,1,0:T(8,128)(2,1)S(1)}, bf16[1,32,400]{2,1,0:T(8,128)(2,1)S(1)}, u32[]{:S(2)}, u32[]{:S(2)}) collective-permute-start(bf16[1,32,400]{2,1,0:T(8,128)(2,1)S(1)} %get-tuple-element.258), channel_id=1, source_target_pairs={{1,0},{2,1},{3,2},{5,4},{6,5},{7,6},{9,8},{10,9},{11,10},{13,12},{... | collective-permute-start | bytes 76808 | tf_op jit(solution)/shard_map/ppermute | solution.py:21
  72.6 7.6 collective-permute-start.8
  92.6 8.7 %collective-permute-start.12 = (bf16[1,32,400]{2,1,0:T(8,128)(2,1)S(1)}, bf16[1,32,400]{2,1,0:T(8,128)(2,1)S(1)}, u32[]{:S(2)}, u32[]{:S(2)}) collective-permute-start(bf16[1,32,400]{2,1,0:T(8,128)(2,1)S(1)} %get-tuple-element.254), channel_id=1, source_target_pairs={{1,0},{2,1},{3,2},{5,4},{6,5},{7,6},{9,8},{10,9},{11,10},{13,12},{... | collective-permute-start | bytes 76808 | tf_op jit(solution)/shard_map/ppermute | solution.py:21
  93.9 7.4 collective-permute-start.11
  125.2 7.5 collective-permute-start.15
  126.4 6.8 collective-permute-start.14
  153.3 7.6 collective-permute-start.17
  158.1 7.0 collective-permute-start.16
  187.1 6.9 collective-permute-start.20
  192.0 6.1 collective-permute-start.19
  211.9 5.2 collective-permute-start.21
  224.3 6.1 collective-permute-start.22
  256.2 6.1 collective-permute-start.25
  284.5 20.5 %collective-permute-start.29 = (bf16[1,32,400]{2,1,0:T(8,128)(2,1)}, bf16[1,32,400]{2,1,0:T(8,128)(2,1)S(1)}, u32[]{:S(2)}, u32[]{:S(2)}) collective-permute-start(bf16[1,32,400]{2,1,0:T(8,128)(2,1)} %get-tuple-element.230), channel_id=1, source_target_pairs={{0,1},{1,2},{2,3},{4,5},{5,6},{6,7},{8,9},{9,10},{10,11},{12,13},{... | collective-permute-start | bytes 76808 | tf_op jit(solution)/shard_map/ppermute | solution.py:20
  287.3 17.8 %collective-permute-start.28 = (bf16[1,32,400]{2,1,0:T(8,128)(2,1)}, bf16[1,32,400]{2,1,0:T(8,128)(2,1)}, u32[]{:S(2)}, u32[]{:S(2)}) collective-permute-start(bf16[1,32,400]{2,1,0:T(8,128)(2,1)} %get-tuple-element.231), channel_id=1, source_target_pairs={{1,0},{2,1},{3,2},{5,4},{6,5},{7,6},{9,8},{10,9},{11,10},{13,12},{... | collective-permute-start | bytes 76808 | tf_op jit(solution)/shard_map/ppermute | solution.py:21
  605.4 43.8 %reduce-scatter.7.cloned.1.call-start = ((), (), s32[]{:S(2)}) async-start(), calls=%async_computation.2 | async-start | bytes 2457600
  621.7 157.4 %all-reduce.6.cloned.1.call-start = ((), (), s32[]{:S(2)}) async-start(), calls=%async_computation.4 | async-start | bytes 5734400 | tf_op jit(solution)/shard_map/psum | solution.py:300
  (276 other events, 1477.5 us)
Sparse Core Ops, SparseCore 0:
  605.5 10.1 reduce-scatter.8
  621.9 10.6 reduce-scatter.6
Sparse Core Ops, SparseCore 1:
  636.2 142.9 all-reduce.5
where the time goes:
time: 802 us; the launch traced here: 791 us
  blocking collectives  279 us (35%)
  waiting for transfers between devices  141 us (18%)
  other arithmetic  101 us (13%)
  matrix products  87.6 us (11%)
  local copies, waits for them, and re-layouts  85.4 us (11%)
  starting transfers between devices  77.3 us (10%)
  between operations  19.6 us (2%)
    psum x1, blocking collectives, per_device(): lax.psum((grad_in_gain, grad_in_shift, grad_down_weight, grad_down_bias,...  279 us
    psum x1, waiting for transfers between devices, per_device(): lax.psum((grad_in_gain, grad_in_shift, grad_down_weight, grad_down_bias,...  124 us
    ppermute x11, starting transfers between devices, extended_2(): before = lax.ppermute(last, axis, up)  50.6 us
    unnamed x557, local copies, waits for them, and re-layouts  48.5 us
    unnamed x22, other arithmetic  26.2 us
    mul x20, other arithmetic, windows(): pieces.append(piece * tap_masks[which][..., None])  20.5 us
    concatenate x10, local copies, waits for them, and re-layouts, windows(): return jnp.concatenate(pieces, axis=-1)  19.1 us
    dot_general x5, matrix products, block_backward(): jnp.einsum('rtk,kh->rth', back_windows, kernel_cols, preferred_element_ty...  16.7 us
  transfers between devices with their start and end apart: 33, of which 7 were waited for; matrix products, arithmetic and copies ran while one was open for 13% of the time, Pallas kernels for 0%

commit v1 on v0

v1 whole, which is shorter than its diff:
```python
import functools

import jax
import jax.numpy as jnp
from jax import lax
from jax.experimental import pallas as pl
from jax.experimental.pallas import tpu as pltpu
from jax.sharding import PartitionSpec as P

DILATION = 16
MARGIN = 2 * DILATION
EPSILON = 1e-05
MESH = pl.DeviceIdType.MESH
BF16 = jnp.bfloat16
F32 = jnp.float32
OFFSETS = (-2 * DILATION, -DILATION, DILATION, 2 * DILATION)
ROOT = 0.7978845608028654
CUBIC = 0.044715 * ROOT
VMEM_LIMIT = 60 * 2**20


def dot(left, right, left_dim, right_dim):
    return lax.dot_general(
        left, right, (((left_dim,), (right_dim,)), ((), ())), preferred_element_type=F32
    )


def across(column, width):
    whole, rest = divmod(width, 128)
    pieces = [column] * whole
    if rest:
        pieces.append(column[:, :rest])
    return jnp.concatenate(pieces, axis=1) if len(pieces) > 1 else pieces[0]


def norm_act(values, gain, shift):
    scale = 1.0 / values.shape[-1]
    centred = values - jnp.sum(values, axis=-1, keepdims=True) * scale
    variance = jnp.sum(centred * centred, axis=-1, keepdims=True) * scale
    factor = lax.rsqrt(variance + EPSILON)
    normed = centred * factor
    pre = normed * gain + shift
    square = pre * pre
    half = 0.5 + 0.5 * jnp.tanh(pre * (ROOT + CUBIC * square))
    act = pre * half
    slope = half + act * (1.0 - half) * (2.0 * ROOT + 6.0 * CUBIC * square)
    return normed, factor, act, slope


def norm_act_back(upstream, slope, normed, factor, gain):
    scale = 1.0 / normed.shape[-1]
    at_pre = upstream * slope
    shift_grad = jnp.sum(at_pre, axis=0, keepdims=True)
    gain_grad = jnp.sum(at_pre * normed, axis=0, keepdims=True)
    scaled = at_pre * gain
    first = jnp.sum(scaled, axis=-1, keepdims=True) * scale
    second = jnp.sum(scaled * normed, axis=-1, keepdims=True) * scale
    return factor * (scaled - first - normed * second), gain_grad, shift_grad


def row_block(rows):
    best = 16
    for size in range(16, 257, 16):
        if rows % size == 0:
            best = size
    return best


class Plan:
    def __init__(self, mesh, rows, length, width, inner, enc_taps, dec_taps):
        self.rows, self.length, self.width, self.inner = rows, length, width, inner
        self.half = rows // 2
        self.tokens = self.half * length
        self.taps = (enc_taps, dec_taps)
        self.n_dp, self.n_seq = mesh.shape["dp"], mesh.shape["seq"]
        self.ext = length + 2 * MARGIN
        self.up_main, self.up_rest = divmod(width, 128)
        self.in_main, self.in_rest = divmod(inner, 128)
        lanes = lambda size: -(-size // 128)
        self.in_tiles, self.width_tiles = lanes(inner), lanes(width)
        self.up_rows = self.up_main * inner + self.up_rest * self.in_tiles
        self.down_rows = self.in_main * width + self.in_rest * self.width_tiles
        self.tap_rows = self.in_main * inner + self.in_rest * self.in_tiles
        position = 0
        self.at = {}
        ready = []
        parts = (
            (("up", 1, self.up_rows),),
            (("kernel", 1, self.tap_rows * dec_taps),),
            (("down", 1, self.down_rows), ("up", 0, self.up_rows)),
            (("kernel", 0, self.tap_rows * enc_taps),),
            (("down", 0, self.down_rows),),
        )
        for group in parts:
            for name, block, size in group:
                self.at[name, block] = position
                position += size
            ready.append(position)
        stages = [("section", (1, 1), 2)]
        bits = self.n_seq.bit_length() - 1
        assert self.n_seq == 1 << bits
        for bit in range(bits):
            stages.append(("seq", (1 << bit, 1 << (bits - 1 - bit)), 2))
        left, stride = self.n_dp, 1
        while left > 1:
            radix = 4 if left % 4 == 0 else 2
            assert left % radix == 0
            stages.append(("dp", (stride, stride), radix))
            left, stride = left // radix, stride * radix
        self.stages = stages
        unit = 16
        for _, _, radix in stages:
            unit *= radix
        edges = [0] + [size // unit * unit for size in ready[:-1]] + [-(-ready[-1] // unit) * unit]
        self.chunks = list(zip(edges[:-1], edges[1:]))
        self.pool_rows = edges[-1]
        self.used_rows = ready[-1]


def main_kernel(plan, *refs):
    (
        blocks_in, cot_in, seg_in, in_gain, in_shift, down_in, down_bias, mid_gain, mid_shift,
        enc_in, dec_in, conv_bias, out_gain, out_shift, up_in, up_bias,
        blocks_out, grads_out, pool_out, vec_out,
        xin, cot, wd, wu, ek, dk, vec, seg_side, masks,
        n1, s1, q1, n2, s2, q2, n3, s3, q3, fa, mid, win, la, outv, cp, hp, gin,
        pool, summed, vsum, vrecv,
        load_sem, pair_send, pair_recv, seg_send, seg_recv, halo_send, halo_recv,
        rs_send, rs_recv, ag_send, ag_recv, vec_send, vec_recv, out_sem, out_send, out_recv,
        *recv_bufs,
    ) = refs
    length, width, inner, half = plan.length, plan.width, plan.inner, plan.half
    kernels = (ek, dk)
    sec = lax.axis_index("section")
    seq = lax.axis_index("seq")
    other = 1 - sec
    other_core = {"section": other}
    right = {"seq": lax.rem(seq + 1, plan.n_seq)}
    left = {"seq": lax.rem(seq + plan.n_seq - 1, plan.n_seq)}
    later_sends = []

    def remote(src, dst, send, recv, device):
        return pltpu.make_async_remote_copy(
            src_ref=src, dst_ref=dst, send_sem=send, recv_sem=recv,
            device_id=device, device_id_type=MESH,
        )

    own_rows = pl.ds(sec * half, half)
    other_rows = pl.ds(other * half, half)
    loads = [
        pltpu.make_async_copy(blocks_in.at[0, own_rows], xin.at[sec], load_sem.at[0]),
        pltpu.make_async_copy(down_in.at[0], wd.at[sec], load_sem.at[1]),
        pltpu.make_async_copy(up_in.at[0], wu.at[sec], load_sem.at[2]),
        pltpu.make_async_copy(enc_in, ek, load_sem.at[3]),
        pltpu.make_async_copy(dec_in, dk, load_sem.at[4]),
        pltpu.make_async_copy(cot_in.at[own_rows], cot, load_sem.at[5]),
    ]
    for load in loads:
        load.start()
    vec[...] = jnp.zeros_like(vec)
    for at, ref in enumerate((in_gain, in_shift, up_bias)):
        vec[sec, at : at + 1, :] = ref[...]
    for at, ref in enumerate((down_bias, mid_gain, mid_shift, conv_bias, out_gain, out_shift)):
        vec[sec, 3 + at : 4 + at, :inner] = ref[...]
    vsum[...] = jnp.zeros_like(vsum)

    digits, peers = [], []
    for axis, strides, radix in plan.stages:
        index = lax.axis_index(axis)
        stride = strides[0] if strides[0] == strides[1] else jnp.where(sec == 0, *strides)
        digit = lax.rem(lax.div(index, stride), radix)
        digits.append(digit)
        peers.append(
            [
                {axis: index + (lax.rem(digit + step, radix) - digit) * stride}
                for step in range(1, radix)
            ]
        )
    greeted = [left, right] + [peer for group in peers for peer in group]
    barrier = pltpu.get_barrier_semaphore()
    for peer in greeted:
        pl.semaphore_signal(barrier, inc=1, device_id=peer, device_id_type=MESH)
    pl.semaphore_wait(barrier, len(greeted))

    pair = [
        remote(blocks_in.at[0, other_rows], xin.at[sec], pair_send.at[0], pair_recv.at[0], other_core),
        remote(vec.at[sec], vec.at[sec], pair_send.at[1], pair_recv.at[1], other_core),
        remote(down_in.at[0], wd.at[sec], pair_send.at[2], pair_recv.at[2], other_core),
        remote(up_in.at[0], wu.at[sec], pair_send.at[3], pair_recv.at[3], other_core),
    ]
    arriving = [
        remote(ref.at[other], ref.at[other], pair_send.at[at], pair_recv.at[at], other_core)
        for at, ref in enumerate((xin, vec, wd, wu))
    ]
    for copy in pair:
        copy.start()
    later_sends.extend(pair)
    seg_copies = [
        remote(seg_in, seg_side.at[0], seg_send.at[0], seg_recv.at[0], right),
        remote(seg_in, seg_side.at[1], seg_send.at[1], seg_recv.at[1], left),
    ]
    for copy in seg_copies:
        copy.start()
    later_sends.extend(seg_copies)

    def wait_block(block):
        @pl.when(sec == block)
        def _():
            for load in loads[:3]:
                load.wait()

        @pl.when(sec != block)
        def _():
            for copy in arriving:
                copy.wait_recv()

    def build_masks():
        for copy in seg_copies:
            copy.wait_recv()
        ext = plan.ext
        place = lax.broadcasted_iota(jnp.int32, (ext, length), 0)
        token = lax.broadcasted_iota(jnp.int32, (ext, length), 1)
        for row in range(half):
            at = pl.ds(sec * half + row, 1)
            own = (seg_in[at, :] + 1).astype(F32)
            before = jnp.where(seq > 0, (seg_side[0, at, :] + 1).astype(F32), 0.0)
            after = jnp.where(seq < plan.n_seq - 1, (seg_side[1, at, :] + 1).astype(F32), 0.0)
            spread = jnp.where(place - MARGIN == token, own, 0.0)
            spread = spread + jnp.where(place + (length - MARGIN) == token, before, 0.0)
            spread = spread + jnp.where(place - (length + MARGIN) == token, after, 0.0)
            numbers = dot(spread.astype(BF16), jnp.ones((length, 128), BF16), 1, 0)
            here = numbers[MARGIN : MARGIN + length]
            for at_offset, offset in enumerate(OFFSETS):
                there = numbers[MARGIN + offset : MARGIN + offset + length]
                masks[at_offset, row] = jnp.where(there == here, 1.0, 0.0).astype(BF16)

    def window(ext_ref, block, row, offset):
        piece = ext_ref[block, row, MARGIN + offset : MARGIN + offset + length, :]
        if offset == 0:
            return piece
        return piece * across(masks[OFFSETS.index(offset), row], inner)

    def params(block):
        wide = [vec[block, at : at + 1, :] for at in range(3)]
        narrow = [vec[block, 3 + at : 4 + at, :inner] for at in range(6)]
        return wide + narrow

    def token_rows(row):
        return pl.ds(pl.multiple_of(row * length, length), length)

    def halo(ref, which, block, row):
        copies = []
        if block == 0 or which == 0:
            copies.append(remote(
                ref.at[block, row, pl.ds(length, MARGIN)], ref.at[block, row, pl.ds(0, MARGIN)],
                halo_send.at[which, block, row, 0], halo_recv.at[which, block, row, 0], right,
            ))
        if block == 0 or which == 1:
            copies.append(remote(
                ref.at[block, row, pl.ds(MARGIN, MARGIN)], ref.at[block, row, pl.ds(length + MARGIN, MARGIN)],
                halo_send.at[which, block, row, 1], halo_recv.at[which, block, row, 1], left,
            ))
        return copies

    def each_row(body):
        def step(row, carry):
            body(row)
            return carry

        lax.fori_loop(0, half, step, 0)

    def entry(block, row):
        values = xin[block, row].astype(F32)
        if block == 1:
            values = values + outv[0, token_rows(row)].astype(F32)
        return values

    def forward_in(block):
        p = params(block)

        def body(row):
            at = token_rows(row)
            normed, factor, act, slope = norm_act(entry(block, row), p[0], p[1])
            n1[block, at] = normed
            s1[block, at] = slope
            q1[block, at] = jnp.broadcast_to(factor, (length, 128))
            act = act.astype(BF16)
            fa[block, at] = act
            hidden = dot(act, wd[block], 1, 0) + p[3]
            normed, factor, act, slope = norm_act(hidden, p[4], p[5])
            n2[block, at] = normed
            s2[block, at] = slope
            q2[block, at] = jnp.broadcast_to(factor, (length, 128))
            mid[block, row, MARGIN : MARGIN + length, :] = act.astype(BF16)
            for copy in halo(mid, 0, block, row):
                copy.start()

        each_row(body)

    def forward_out(block):
        p = params(block)

        def body(row):
            at = token_rows(row)
            for copy in halo(mid, 0, block, row):
                copy.wait()
            total = None
            for tap in range(plan.taps[block]):
                piece = window(mid, block, row, (tap - 2) * DILATION)
                win[block, tap, at] = piece
                term = dot(piece, kernels[block][tap], 1, 0)
                total = term if total is None else total + term
            normed, factor, act, slope = norm_act(total + p[6], p[7], p[8])
            n3[block, at] = normed
            s3[block, at] = slope
            q3[block, at] = jnp.broadcast_to(factor, (length, 128))
            act = act.astype(BF16)
            la[block, at] = act
            result = entry(block, row) + dot(act, wu[block], 1, 0) + p[2]
            outv[block, at] = result.astype(BF16)

        each_row(body)

    def add_wide(block, at, value):
        vsum[block, 0, at : at + 1, :] += value[:, :512]
        vsum[block, 0, at + 1 : at + 2, : width - 512] += value[:, 512:]

    def add_narrow(block, at, value):
        vsum[block, 0, at : at + 1, :inner] += value

    def upstream_of(block, row):
        return cot[row] if block == 1 else gin[1, token_rows(row)]

    def backward_out(block):
        p = params(block)

        def body(row):
            at = token_rows(row)
            incoming = upstream_of(block, row)
            add_wide(block, 4, jnp.sum(incoming.astype(F32), axis=0, keepdims=True))
            d_last = dot(incoming, wu[block], 1, 1)
            d_conv, gain_grad, shift_grad = norm_act_back(
                d_last, s3[block, at], n3[block, at], across(q3[block, at], inner), p[7]
            )
            add_narrow(block, 10, gain_grad)
            add_narrow(block, 11, shift_grad)
            add_narrow(block, 9, jnp.sum(d_conv, axis=0, keepdims=True))
            cp[block, row, MARGIN : MARGIN + length, :] = d_conv.astype(BF16)
            for copy in halo(cp, 1, block, row):
                copy.start()

        each_row(body)

    def backward_in(block):
        p = params(block)

        def body(row):
            at = token_rows(row)
            for copy in halo(cp, 1, block, row):
                copy.wait()
            total = None
            for tap in range(plan.taps[block]):
                piece = window(cp, block, row, -(tap - 2) * DILATION)
                term = dot(piece, kernels[block][tap], 1, 1)
                total = term if total is None else total + term
            d_hidden, gain_grad, shift_grad = norm_act_back(
                total, s2[block, at], n2[block, at], across(q2[block, at], inner), p[4]
            )
            add_narrow(block, 7, gain_grad)
            add_narrow(block, 8, shift_grad)
            add_narrow(block, 6, jnp.sum(d_hidden, axis=0, keepdims=True))
            d_hidden = d_hidden.astype(BF16)
            hp[block, at] = d_hidden
            d_first = dot(d_hidden, wd[block], 1, 1)
            d_entry, gain_grad, shift_grad = norm_act_back(
                d_first, s1[block, at], n1[block, at], across(q1[block, at], width), p[0]
            )
            add_wide(block, 0, gain_grad)
            add_wide(block, 2, shift_grad)
            gin[block, at] = (upstream_of(block, row).astype(F32) + d_entry).astype(BF16)

        each_row(body)

    def to_pool(position, left_value, right_value):
        rows, columns = left_value.shape[1], right_value.shape[1]
        main, rest = divmod(columns, 128)
        product = dot(left_value, right_value[:, : main * 128], 0, 0).astype(BF16)
        for tile in range(main):
            pool[position + tile * rows : position + (tile + 1) * rows, :] = product[
                :, tile * 128 : (tile + 1) * 128
            ]
        position += main * rows
        product = dot(right_value[:, main * 128 :], left_value, 0, 0).astype(BF16)
        for tile in range(-(-rows // 128)):
            lanes = min(128, rows - tile * 128)
            pool[position + tile * rest : position + (tile + 1) * rest, :lanes] = product[
                :, tile * 128 : tile * 128 + lanes
            ]

    def upstream_all(block):
        return jnp.concatenate([upstream_of(block, row) for row in range(half)], axis=0)

    def up_weight_grad(block):
        to_pool(plan.at["up", block], la[block], upstream_all(block))

    def kernel_grad(block):
        grad = jnp.concatenate(
            [cp[block, row, MARGIN : MARGIN + length, :] for row in range(half)], axis=0
        )
        for tap in range(plan.taps[block]):
            to_pool(plan.at["kernel", block] + tap * plan.tap_rows, win[block, tap], grad)

    def down_weight_grad(block):
        to_pool(plan.at["down", block], fa[block], hp[block])

    def shape_of(chunk):
        first, last = plan.chunks[chunk]
        sizes, starts, offsets = [last - first], [first], [first]
        for digit, (_, _, radix) in zip(digits, plan.stages):
            sizes.append(sizes[-1] // radix)
            starts.append(starts[-1] // radix)
            offsets.append(pl.multiple_of(offsets[-1] + digit * sizes[-1], 16))
        return sizes, starts, offsets

    def rs_start(chunk, stage):
        sizes, starts, offsets = shape_of(chunk)
        size, radix = sizes[stage + 1], plan.stages[stage][2]
        for step in range(1, radix):
            part = lax.rem(digits[stage] + step, radix)
            copy = remote(
                pool.at[pl.ds(pl.multiple_of(offsets[stage] + part * size, 16), size)],
                recv_bufs[stage].at[step - 1, pl.ds(starts[stage + 1], size)],
                rs_send.at[chunk, stage, step - 1], rs_recv.at[chunk, stage, step - 1],
                peers[stage][step - 1],
            )
            copy.start()
            later_sends.append(copy)

    def rs_finish(chunk, stage):
        sizes, starts, offsets = shape_of(chunk)
        size, radix = sizes[stage + 1], plan.stages[stage][2]
        for step in range(1, radix):
            slot = recv_bufs[stage].at[step - 1, pl.ds(starts[stage + 1], size)]
            remote(
                slot, slot, rs_send.at[chunk, stage, step - 1], rs_recv.at[chunk, stage, step - 1],
                peers[stage][step - 1],
            ).wait_recv()
        block = row_block(size)
        target = summed if stage + 1 == len(plan.stages) else pool

        def add(at, carry):
            own = pl.ds(pl.multiple_of(offsets[stage + 1] + at * block, 16), block)
            landed = pl.ds(pl.multiple_of(starts[stage + 1] + at * block, 16), block)
            total = pool[own, :].astype(F32)
            for step in range(1, radix):
                total = total + recv_bufs[stage][step - 1, landed, :].astype(F32)
            target[own, :] = total.astype(BF16)
            return carry

        lax.fori_loop(0, size // block, add, 0)

    def ag_start(chunk, stage):
        sizes, starts, offsets = shape_of(chunk)
        part = summed.at[pl.ds(offsets[stage + 1], sizes[stage + 1])]
        for step in range(1, plan.stages[stage][2]):
            copy = remote(
                part, part, ag_send.at[chunk, stage, step - 1], ag_recv.at[chunk, stage, step - 1],
                peers[stage][step - 1],
            )
            copy.start()
            later_sends.append(copy)

    def ag_finish(chunk, stage):
        sizes, starts, offsets = shape_of(chunk)
        size, radix = sizes[stage + 1], plan.stages[stage][2]
        for step in range(1, radix):
            sender = lax.rem(digits[stage] + radix - step, radix)
            part = summed.at[pl.ds(pl.multiple_of(offsets[stage] + sender * size, 16), size)]
            remote(
                part, part, ag_send.at[chunk, stage, step - 1], ag_recv.at[chunk, stage, step - 1],
                peers[stage][step - 1],
            ).wait_recv()

    pool_copies = []

    def pool_done(chunk):
        first, last = plan.chunks[chunk]
        copy = pltpu.make_async_copy(
            summed.at[pl.ds(first, last - first)], pool_out.at[pl.ds(first, last - first)], out_sem.at[chunk]
        )
        copy.start()
        pool_copies.append(copy)

    def chunk_events(chunk):
        if plan.chunks[chunk][0] == plan.chunks[chunk][1]:
            return
        count = len(plan.stages)
        for stage in range(count):
            rs_start(chunk, stage)
            yield
            rs_finish(chunk, stage)
        for stage in reversed(range(count)):
            ag_start(chunk, stage)
            yield
            ag_finish(chunk, stage)
        pool_done(chunk)

    def vector_events(block):
        for stage, (_, _, radix) in enumerate(plan.stages):
            for step in range(1, radix):
                copy = remote(
                    vsum.at[block, stage], vrecv.at[block, stage, step - 1],
                    vec_send.at[block, stage, step - 1], vec_recv.at[block, stage, step - 1],
                    peers[stage][step - 1],
                )
                copy.start()
                later_sends.append(copy)
            yield
            total = vsum[block, stage]
            for step in range(1, radix):
                slot = vrecv.at[block, stage, step - 1]
                remote(
                    slot, slot, vec_send.at[block, stage, step - 1],
                    vec_recv.at[block, stage, step - 1], peers[stage][step - 1],
                ).wait_recv()
                total = total + vrecv[block, stage, step - 1]
            vsum[block, stage + 1] = total

    running = []

    def begin(events):
        if next(events, "done") != "done":
            running.append(events)

    def tick():
        for events in list(running):
            if next(events, "done") == "done":
                running.remove(events)

    wait_block(0)
    build_masks()
    forward_in(0)
    loads[3].wait()
    forward_out(0)
    wait_block(1)
    loads[4].wait()
    loads[5].wait()
    forward_in(1)
    forward_out(1)
    up_weight_grad(1)
    begin(chunk_events(0))
    backward_out(1)
    tick()
    kernel_grad(1)
    begin(chunk_events(1))
    tick()
    backward_in(1)
    tick()
    down_weight_grad(1)
    up_weight_grad(0)
    begin(chunk_events(2))
    begin(vector_events(1))
    tick()
    backward_out(0)
    tick()
    kernel_grad(0)
    begin(chunk_events(3))
    tick()
    backward_in(0)
    tick()
    down_weight_grad(0)
    if plan.pool_rows > plan.used_rows:
        pool[plan.used_rows : plan.pool_rows, :] = jnp.zeros(
            (plan.pool_rows - plan.used_rows, 128), BF16
        )
    begin(chunk_events(4))
    begin(vector_events(0))

    copies = []
    for at, (value, result) in enumerate(((outv, blocks_out), (gin, grads_out))):
        for row in range(half):
            rows = pl.ds(row * length, length)
            target = result.at[0, sec * half + row]
            landing = result.at[0, other * half + row]
            copies.append((
                pltpu.make_async_copy(value.at[sec, rows], target, out_send.at[0, at, row]),
                remote(value.at[other, rows], target, out_send.at[1, at, row], out_recv.at[at, row], other_core),
                remote(value.at[other, rows], landing, out_send.at[1, at, row], out_recv.at[at, row], other_core),
            ))
    for local, away, _ in copies:
        local.start()
        away.start()
    while running:
        tick()
    vec_out[...] = vsum[sec, len(plan.stages)]
    for local, away, arrives in copies:
        local.wait()
        away.wait_send()
        arrives.wait_recv()
    for copy in pool_copies:
        copy.wait()
    for copy in later_sends:
        copy.wait_send()


def final_kernel(plan, blocks_in, grads_in, pool_in, vec, *refs):
    (
        blocks_out, grads_out, g_in_gain, g_in_shift, g_down, g_down_bias, g_mid_gain, g_mid_shift,
        g_enc, g_dec, g_conv_bias, g_out_gain, g_out_shift, g_up, g_up_bias,
        up_pool, down_pool, tap_pool, up_full, down_full, enc_full, dec_full,
        in_sem, out_sem,
    ) = refs
    sec = lax.axis_index("section")
    width, inner = plan.width, plan.inner
    passed = [
        pltpu.make_async_copy(blocks_in, blocks_out, out_sem.at[0]),
        pltpu.make_async_copy(grads_in, grads_out, out_sem.at[1]),
    ]
    for copy in passed:
        copy.start()

    def load(name, target, size, sem):
        start = jnp.where(sec == 0, plan.at[name, 0], plan.at[name, 1])
        copy = pltpu.make_async_copy(pool_in.at[pl.ds(pl.multiple_of(start, 16), size)], target, in_sem.at[sem])
        copy.start()
        return copy

    up_load = load("up", up_pool, plan.up_rows, 0)
    down_load = load("down", down_pool, plan.down_rows, 1)
    tap_loads = []
    at = 0
    for block in (0, 1):
        size = plan.tap_rows * plan.taps[block]
        start = plan.at["kernel", block]
        copy = pltpu.make_async_copy(pool_in.at[pl.ds(start, size)], tap_pool.at[pl.ds(at, size)], in_sem.at[2 + block])
        copy.start()
        tap_loads.append(copy)
        at += size

    def wide(at):
        return jnp.concatenate([vec[at : at + 1, :], vec[at + 1 : at + 2, : width - 512]], axis=1)

    g_in_gain[...] = wide(0)
    g_in_shift[...] = wide(2)
    g_up_bias[...] = wide(4)
    for at, ref in enumerate((g_down_bias, g_mid_gain, g_mid_shift, g_conv_bias, g_out_gain, g_out_shift)):
        ref[...] = vec[6 + at : 7 + at, :inner]

    def rest_of(ref, position, rest, tiles):
        pieces = [ref[position + tile * rest : position + (tile + 1) * rest, :] for tile in range(tiles)]
        return jnp.concatenate(pieces, axis=1).astype(F32)

    def unpack(ref, full, rows, main, rest, tiles):
        for tile in range(main):
            full[:, tile * 128 : (tile + 1) * 128] = ref[tile * rows : (tile + 1) * rows, :].astype(F32)
        left = rest_of(ref, main * rows, rest, tiles)
        full[:, main * 128 :] = left.T[:rows, :]

    up_load.wait()
    unpack(up_pool, up_full, inner, plan.up_main, plan.up_rest, plan.in_tiles)
    up_store = pltpu.make_async_copy(up_full, g_up.at[0], out_sem.at[2])
    up_store.start()
    down_load.wait()
    unpack(down_pool, down_full, width, plan.in_main, plan.in_rest, plan.width_tiles)
    down_store = pltpu.make_async_copy(down_full, g_down.at[0], out_sem.at[3])
    down_store.start()
    part = inner // 2
    row = lax.broadcasted_iota(jnp.int32, (inner, part), 0)
    column = lax.broadcasted_iota(jnp.int32, (inner, part), 1)
    choose = jnp.where(row == column + sec * part, 1.0, 0.0).astype(BF16)
    stores = []
    at = 0
    for block, full, target in ((0, enc_full, g_enc), (1, dec_full, g_dec)):
        tap_loads[block].wait()
        for tap in range(plan.taps[block]):
            main = jnp.concatenate(
                [tap_pool[at + tile * inner : at + (tile + 1) * inner, :] for tile in range(plan.in_main)], axis=1
            )
            lanes = plan.in_main * 128
            rest = rest_of(tap_pool, at + plan.in_main * inner, plan.in_rest, plan.in_tiles)
            rest = rest[:, :inner].astype(BF16)
            full[tap] = dot(main, choose[:lanes], 1, 0) + dot(rest, choose[lanes:], 0, 0)
            at += plan.tap_rows
        copy = pltpu.make_async_copy(full, target, out_sem.at[4 + block])
        copy.start()
        stores.append(copy)
    for copy in passed + [up_store, down_store] + stores:
        copy.wait()


def per_device(plan, *args):
    (
        block_inputs, cotangent, segment_ids, in_gain, in_shift, down_weight, down_bias, mid_gain,
        mid_shift, enc_kernel, dec_kernel, conv_bias, out_gain, out_shift, up_weight, up_bias,
    ) = args
    length, width, inner, half, tokens = plan.length, plan.width, plan.inner, plan.half, plan.tokens
    stages = len(plan.stages)
    most = max(radix for _, _, radix in plan.stages) - 1
    chunks = len(plan.chunks)
    any_spec = pl.BlockSpec(memory_space=pl.ANY)
    vmem_spec = pl.BlockSpec(memory_space=pltpu.VMEM)
    wide = lambda kind: pltpu.VMEM((2, tokens, width), kind)
    narrow = lambda kind: pltpu.VMEM((2, tokens, inner), kind)
    factor = pltpu.VMEM((2, tokens, 128), F32)
    dma = pltpu.SemaphoreType.DMA
    recv_bufs, left = [], plan.pool_rows
    for _, _, radix in plan.stages:
        left //= radix
        recv_bufs.append(pltpu.VMEM((radix - 1, left, 128), BF16))
    enc_taps, dec_taps = plan.taps
    blocks, grads, pool, vectors = pl.pallas_call(
        functools.partial(main_kernel, plan),
        out_shape=(
            jax.ShapeDtypeStruct(block_inputs.shape, BF16),
            jax.ShapeDtypeStruct(block_inputs.shape, BF16),
            jax.ShapeDtypeStruct((plan.pool_rows, 128), BF16),
            jax.ShapeDtypeStruct((16, 512), F32),
        ),
        in_specs=[any_spec, any_spec, vmem_spec, vmem_spec, vmem_spec, any_spec, vmem_spec, vmem_spec,
                  vmem_spec, any_spec, any_spec, vmem_spec, vmem_spec, vmem_spec, any_spec, vmem_spec],
        out_specs=(any_spec, any_spec, any_spec, vmem_spec),
        scratch_shapes=[
            pltpu.VMEM((2, half, length, width), BF16),
            pltpu.VMEM((half, length, width), BF16),
            pltpu.VMEM((2, width, inner), BF16),
            pltpu.VMEM((2, inner, width), BF16),
            pltpu.VMEM((enc_taps, inner, inner), BF16),
            pltpu.VMEM((dec_taps, inner, inner), BF16),
            pltpu.VMEM((2, 16, width), F32),
            pltpu.VMEM((2,) + segment_ids.shape, jnp.int32),
            pltpu.VMEM((len(OFFSETS), half, length, 128), BF16),
            wide(F32), wide(F32), factor,
            narrow(F32), narrow(F32), factor,
            narrow(F32), narrow(F32), factor,
            wide(BF16),
            pltpu.VMEM((2, half, plan.ext, inner), BF16),
            pltpu.VMEM((2, enc_taps, tokens, inner), BF16),
            narrow(BF16),
            wide(BF16),
            pltpu.VMEM((2, half, plan.ext, inner), BF16),
            narrow(BF16),
            wide(BF16),
            pltpu.VMEM((plan.pool_rows, 128), BF16),
            pltpu.VMEM((plan.pool_rows, 128), BF16),
            pltpu.VMEM((2, stages + 1, 16, 512), F32),
            pltpu.VMEM((2, stages, most, 16, 512), F32),
            dma((6,)), dma((4,)), dma((4,)), dma((2,)), dma((2,)),
            dma((2, 2, half, 2)), dma((2, 2, half, 2)),
            dma((chunks, stages, most)), dma((chunks, stages, most)),
            dma((chunks, stages, most)), dma((chunks, stages, most)),
            dma((2, stages, most)), dma((2, stages, most)),
            dma((chunks,)), dma((2, 2, half)), dma((2, half)),
        ] + recv_bufs,
        compiler_params=pltpu.CompilerParams(
            collective_id=0, has_side_effects=True, vmem_limit_bytes=VMEM_LIMIT
        ),
        name="blocks_and_sums",
    )(*args)
    vector = lambda size: jax.ShapeDtypeStruct((1, size), F32)
    part = inner // 2
    return pl.pallas_call(
        functools.partial(final_kernel, plan),
        out_shape=(
            jax.ShapeDtypeStruct(block_inputs.shape, BF16),
            jax.ShapeDtypeStruct(block_inputs.shape, BF16),
            vector(width), vector(width),
            jax.ShapeDtypeStruct((1, width, inner), F32),
            vector(inner), vector(inner), vector(inner),
            jax.ShapeDtypeStruct((enc_taps, inner, part), F32),
            jax.ShapeDtypeStruct((dec_taps, inner, part), F32),
            vector(inner), vector(inner), vector(inner),
            jax.ShapeDtypeStruct((1, inner, width), F32),
            vector(width),
        ),
        in_specs=[any_spec, any_spec, any_spec, vmem_spec],
        out_specs=(any_spec, any_spec, vmem_spec, vmem_spec, any_spec, vmem_spec, vmem_spec, vmem_spec,
                   any_spec, any_spec, vmem_spec, vmem_spec, vmem_spec, any_spec, vmem_spec),
        scratch_shapes=[
            pltpu.VMEM((plan.up_rows, 128), BF16),
            pltpu.VMEM((plan.down_rows, 128), BF16),
            pltpu.VMEM((plan.tap_rows * (enc_taps + dec_taps), 128), BF16),
            pltpu.VMEM((inner, width), F32),
            pltpu.VMEM((width, inner), F32),
            pltpu.VMEM((enc_taps, inner, part), F32),
            pltpu.VMEM((dec_taps, inner, part), F32),
            dma((4,)), dma((6,)),
        ],
        compiler_params=pltpu.CompilerParams(vmem_limit_bytes=VMEM_LIMIT),
        name="unpack_sums",
    )(blocks, grads, pool, vectors)


def solution(mesh):
    def whole(*args):
        rows, length, width = (
            args[0].shape[1] // mesh.shape["dp"], args[0].shape[2] // mesh.shape["seq"], args[0].shape[3]
        )
        inner = args[9].shape[1]
        plan = Plan(mesh, rows, length, width, inner, args[9].shape[0], args[10].shape[0])
        by_section = P("section", None)
        weight = P("section", None, None)
        data = P("section", "dp", "seq", None)
        return jax.shard_map(
            functools.partial(per_device, plan),
            mesh=mesh,
            in_specs=(
                data, P("dp", "seq", None), P("dp", "seq"), by_section, by_section, weight, by_section,
                by_section, by_section, P(), P(), by_section, by_section, by_section, weight, by_section,
            ),
            out_specs=(
                data, data, by_section, by_section, weight, by_section, by_section, by_section,
                P(None, None, "section"), P(None, None, "section"),
                by_section, by_section, by_section, weight, by_section,
            ),
            check_vma=False,
        )(*args)

    return whole
```

time: 802 us -> 198 us (0.25); the launches traced: 791 us -> 197 us
  blocking collectives: 279 us -> 0 us
  Pallas kernels: 0 us -> 191 us
  waiting for transfers between devices: 141 us -> 0 us
  other arithmetic: 101 us -> 0 us
  matrix products: 87.6 us -> 0 us
  local copies, waits for them, and re-layouts: 85.4 us -> 5.32 us
  starting transfers between devices: 77.3 us -> 0 us
  between operations: 19.6 us -> 0.66 us
    psum x1 -> x0, blocking collectives: 279 us -> none  [per_device(): lax.psum((grad_in_gain, grad_in_shift, grad_down_weight, grad_down_bias,...]
    pallas_call x0 -> x2, Pallas kernels: none -> 191 us  [the longest x1 105 us: per_device(): pl.pallas_call(functools.partial(main_kernel, plan), out_shape=(jax.Shape...]
    psum x1 -> x0, waiting for transfers between devices: 124 us -> none  [per_device(): lax.psum((grad_in_gain, grad_in_shift, grad_down_weight, grad_down_bias,...]
    dot_general x45 -> x0, matrix products: 87.6 us -> none  [the longest x5 16.7 us: block_backward(): jnp.einsum('rtk,kh->rth', back_windows, kernel_cols, preferred_element_ty...]
    ppermute x30 -> x0, starting transfers between devices: 77 us -> none  [the longest x11 50.6 us: extended_2(): before = lax.ppermute(last, axis, up)]
    unnamed x557 -> x1, local copies, waits for them, and re-layouts: 48.5 us -> 2.28 us
    reduce_sum x35 -> x0, other arithmetic: 31.2 us -> none  [the longest x17 10.1 us: normalize(): variance = jnp.mean(centred * centred, axis=-1, keepdims=True)]
    unnamed x22 -> x0, other arithmetic: 26.2 us -> none
  transfers between devices with their start and end apart: 33 -> 0, of which waited for: 7 -> 0; matrix products, arithmetic and copies ran while one was open for 13% -> 0% of each run, Pallas kernels for 0% -> 0%
where the time goes in v1:
time: 198 us; the launch traced here: 197 us
  Pallas kernels  191 us (96%)
  local copies, waits for them, and re-layouts  5.32 us (3%)
    pallas_call x1, Pallas kernels, per_device(): pl.pallas_call(functools.partial(main_kernel, plan), out_shape=(jax.Shape...  105 us
    pallas_call x1, Pallas kernels, per_device(): pl.pallas_call(functools.partial(final_kernel, plan), out_shape=(jax.Shap...  86 us

profile of v1, /device:TPU:0, one launch (start us, length us, event | category | flops | bytes accessed | tf_op | source)
XLA Modules:
  0.0 197.0 jit_solution(211681008608985493)
XLA Ops:
  0.6 2.3 %copy.31.refs_5_ = bf16[1,800,400]{2,1,0:T(8,128)(2,1)} copy(bf16[1,800,400]{1,2,0:T(8,128)(2,1)} %param.21) | data formatting | bytes 1280000 | tf_op args[5]
  2.9 105.1 %blocks_and_sums.1 = (bf16[1,4,192,800]{3,2,1,0:T(8,128)(2,1)}, bf16[1,4,192,800]{3,2,1,0:T(8,128)(2,1)}, bf16[20480,128]{1,0:T(8,128)(2,1)}, f32[16,512]{1,0:T(8,128)}) custom-call(bf16[1,4,192,800]{3,2,1,0:T(8,128)(2,1)} %refs_0_.1, bf16[4,192,800]{2,1,0:T(8,128)(2,1)} %refs_1_.1, s32[4,192]{1,0:T(4,128)} %refs_2_.1, f32[1,800]{1,0:T(1,128)} %refs_3_.1, ...), custom_call_target="tpu_custom_call" | custom-call | tf_op jit(solution)/shard_map/blocks_and_sums/pallas_call | solution.py:711
  108.0 86.0 %unpack_sums.1 = (bf16[1,4,192,800]{3,2,1,0:T(8,128)(2,1)}, bf16[1,4,192,800]{3,2,1,0:T(8,128)(2,1)}, f32[1,800]{1,0:T(1,128)}, f32[1,800]{1,0:T(1,128)}, f32[1,...) custom-call(bf16[1,4,192,800]{3,2,1,0:T(8,128)(2,1)} %get-tuple-elem, ...), custom_call_target="tpu_custom_call" | custom-call | tf_op jit(solution)/shard_map/unpack_sums/pallas_call | solution.py:761
  194.0 3.0 %copy.32 = f32[1,800,400]{1,2,0:T(8,128)} copy(f32[1,800,400]{2,1,0:T(8,128)} %get-tuple-element.27) | data formatting | bytes 2560000 | tf_op jit(solution)/shard_map/unpack_sums/pallas_call | solution.py:761

commit v2 on v1

--- a/solution.py
+++ b/solution.py
@@ -17,6 +17,7 @@
 ROOT = 0.7978845608028654
 CUBIC = 0.044715 * ROOT
 VMEM_LIMIT = 60 * 2**20
+VECTORS = -1
 
 
 def dot(left, right, left_dim, right_dim):
@@ -64,6 +65,9 @@
         if rows % size == 0:
             best = size
     return best
+
+
+CHUNKS = ((('up', 1, 0), 'direct'), (('kernel', 1, 9), 'std'), (('down', 1, 0), 'std'), (('up', 0, 0), 'std'), (('kernel', 0, 2), 'std'), (('kernel', 0, 9), 'std'), (('down', 0, 0), 'direct'))
 
 
 class Plan:
@@ -79,42 +83,52 @@
         lanes = lambda size: -(-size // 128)
         self.in_tiles, self.width_tiles = lanes(inner), lanes(width)
         self.up_rows = self.up_main * inner + self.up_rest * self.in_tiles
-        self.down_rows = self.in_main * width + self.in_rest * self.width_tiles
+        self.down_rows = self.up_rows
         self.tap_rows = self.in_main * inner + self.in_rest * self.in_tiles
         position = 0
-        self.at = {}
-        ready = []
-        parts = (
-            (("up", 1, self.up_rows),),
-            (("kernel", 1, self.tap_rows * dec_taps),),
-            (("down", 1, self.down_rows), ("up", 0, self.up_rows)),
-            (("kernel", 0, self.tap_rows * enc_taps),),
-            (("down", 0, self.down_rows),),
-        )
-        for group in parts:
-            for name, block, size in group:
-                self.at[name, block] = position
+        self.at, ends = {}, {}
+        for name, block, size, pieces in (
+            ("up", 1, self.up_rows, 1), ("kernel", 1, self.tap_rows, dec_taps), ("down", 1, self.down_rows, 1),
+            ("up", 0, self.up_rows, 1), ("kernel", 0, self.tap_rows, enc_taps), ("down", 0, self.down_rows, 1),
+        ):
+            self.at[name, block] = position
+            for piece in range(pieces):
                 position += size
-            ready.append(position)
-        stages = [("section", (1, 1), 2)]
+                ends[name, block, piece] = position
+        self.used_rows = position
+        section = [("section", (1, 1), 2)]
         bits = self.n_seq.bit_length() - 1
         assert self.n_seq == 1 << bits
-        for bit in range(bits):
-            stages.append(("seq", (1 << bit, 1 << (bits - 1 - bit)), 2))
-        left, stride = self.n_dp, 1
+        halves = [("seq", (1 << bit, 1 << (bits - 1 - bit)), 2) for bit in range(bits)]
+        direct = [("seq", (1, 1), self.n_seq)] if bits else []
+        layers, left, stride = [], self.n_dp, 1
         while left > 1:
             radix = 4 if left % 4 == 0 else 2
             assert left % radix == 0
-            stages.append(("dp", (stride, stride), radix))
+            layers.append(("dp", (stride, stride), radix))
             left, stride = left // radix, stride * radix
-        self.stages = stages
-        unit = 16
-        for _, _, radix in stages:
-            unit *= radix
-        edges = [0] + [size // unit * unit for size in ready[:-1]] + [-(-ready[-1] // unit) * unit]
-        self.chunks = list(zip(edges[:-1], edges[1:]))
-        self.pool_rows = edges[-1]
-        self.used_rows = ready[-1]
+        orders = {"std": section + halves + layers, "dp first": section + layers + halves,
+                  "direct": section + direct + layers}
+        self.vec_stages = orders["direct"]
+        unit = 32 * self.n_seq * self.n_dp
+        self.chunks, first = [], 0
+        for (name, block, piece), order in CHUNKS:
+            last = ends[name, block, min(piece, self.taps[block] - 1)]
+            last = -(-last // unit) * unit if last == self.used_rows else last // unit * unit
+            self.chunks.append((first, last, orders[order]))
+            first = last
+        self.pool_rows = first
+        self.landing, self.recv_rows = [], 0
+        for first, last, stages in self.chunks:
+            size, places = last - first, []
+            for _, _, radix in stages:
+                size //= radix
+                places.append(self.recv_rows)
+                self.recv_rows += size * (radix - 1)
+            self.landing.append(places)
+        self.sent_rows = self.pool_rows - self.pool_rows // (unit // 16)
+        self.most_stages = max(len(stages) for _, _, stages in self.chunks)
+        self.vec_copies = sum(radix - 1 for _, _, radix in self.vec_stages)
 
 
 def main_kernel(plan, *refs):
@@ -124,10 +138,9 @@
         blocks_out, grads_out, pool_out, vec_out,
         xin, cot, wd, wu, ek, dk, vec, seg_side, masks,
         n1, s1, q1, n2, s2, q2, n3, s3, q3, fa, mid, win, la, outv, cp, hp, gin,
-        pool, summed, vsum, vrecv,
+        pool, summed, recv, vsum, vtotal, vrecv,
         load_sem, pair_send, pair_recv, seg_send, seg_recv, halo_send, halo_recv,
-        rs_send, rs_recv, ag_send, ag_recv, vec_send, vec_recv, out_sem, out_send, out_recv,
-        *recv_bufs,
+        pool_send, rs_recv, ag_recv, vec_send, vec_recv, out_sem, out_send, out_recv,
     ) = refs
     length, width, inner, half = plan.length, plan.width, plan.inner, plan.half
     kernels = (ek, dk)
@@ -164,19 +177,22 @@
         vec[sec, 3 + at : 4 + at, :inner] = ref[...]
     vsum[...] = jnp.zeros_like(vsum)
 
-    digits, peers = [], []
-    for axis, strides, radix in plan.stages:
-        index = lax.axis_index(axis)
-        stride = strides[0] if strides[0] == strides[1] else jnp.where(sec == 0, *strides)
-        digit = lax.rem(lax.div(index, stride), radix)
-        digits.append(digit)
-        peers.append(
-            [
+    known = {}
+
+    def place(stage):
+        if stage not in known:
+            axis, strides, radix = stage
+            index = lax.axis_index(axis)
+            stride = strides[0] if strides[0] == strides[1] else jnp.where(sec == 0, *strides)
+            digit = lax.rem(lax.div(index, stride), radix)
+            others = [
                 {axis: index + (lax.rem(digit + step, radix) - digit) * stride}
                 for step in range(1, radix)
             ]
-        )
-    greeted = [left, right] + [peer for group in peers for peer in group]
+            known[stage] = digit, others
+        return known[stage]
+
+    greeted = [peer for stage in plan.vec_stages for peer in place(stage)[1]]
     barrier = pltpu.get_barrier_semaphore()
     for peer in greeted:
         pl.semaphore_signal(barrier, inc=1, device_id=peer, device_id_type=MESH)
@@ -286,7 +302,7 @@
             q1[block, at] = jnp.broadcast_to(factor, (length, 128))
             act = act.astype(BF16)
             fa[block, at] = act
-            hidden = dot(act, wd[block], 1, 0) + p[3]
+            hidden = dot(act, wd[block], 1, 1) + p[3]
             normed, factor, act, slope = norm_act(hidden, p[4], p[5])
             n2[block, at] = normed
             s2[block, at] = slope
@@ -322,11 +338,11 @@
         each_row(body)
 
     def add_wide(block, at, value):
-        vsum[block, 0, at : at + 1, :] += value[:, :512]
-        vsum[block, 0, at + 1 : at + 2, : width - 512] += value[:, 512:]
+        vsum[block, at : at + 1, :] += value[:, :512]
+        vsum[block, at + 1 : at + 2, : width - 512] += value[:, 512:]
 
     def add_narrow(block, at, value):
-        vsum[block, 0, at : at + 1, :inner] += value
+        vsum[block, at : at + 1, :inner] += value
 
     def upstream_of(block, row):
         return cot[row] if block == 1 else gin[1, token_rows(row)]
@@ -351,7 +367,7 @@
 
         each_row(body)
 
-    def backward_in(block):
+    def backward_mid(block):
         p = params(block)
 
         def body(row):
@@ -369,9 +385,16 @@
             add_narrow(block, 7, gain_grad)
             add_narrow(block, 8, shift_grad)
             add_narrow(block, 6, jnp.sum(d_hidden, axis=0, keepdims=True))
-            d_hidden = d_hidden.astype(BF16)
-            hp[block, at] = d_hidden
-            d_first = dot(d_hidden, wd[block], 1, 1)
+            hp[block, at] = d_hidden.astype(BF16)
+
+        each_row(body)
+
+    def backward_in(block):
+        p = params(block)
+
+        def body(row):
+            at = token_rows(row)
+            d_first = dot(hp[block, at], wd[block], 1, 0)
             d_entry, gain_grad, shift_grad = norm_act_back(
                 d_first, s1[block, at], n1[block, at], across(q1[block, at], width), p[0]
             )
@@ -403,139 +426,118 @@
     def up_weight_grad(block):
         to_pool(plan.at["up", block], la[block], upstream_all(block))
 
-    def kernel_grad(block):
+    def kernel_grad(block, tap):
         grad = jnp.concatenate(
             [cp[block, row, MARGIN : MARGIN + length, :] for row in range(half)], axis=0
         )
-        for tap in range(plan.taps[block]):
-            to_pool(plan.at["kernel", block] + tap * plan.tap_rows, win[block, tap], grad)
+        to_pool(plan.at["kernel", block] + tap * plan.tap_rows, win[block, tap], grad)
 
     def down_weight_grad(block):
-        to_pool(plan.at["down", block], fa[block], hp[block])
-
-    def shape_of(chunk):
-        first, last = plan.chunks[chunk]
-        sizes, starts, offsets = [last - first], [first], [first]
-        for digit, (_, _, radix) in zip(digits, plan.stages):
+        to_pool(plan.at["down", block], hp[block], fa[block])
+
+    pool_copies, running = [], {}
+
+    def sum_chunk(chunk):
+        first, last, stages = plan.chunks[chunk]
+        places = [place(stage) for stage in stages]
+        sizes, offsets = [last - first], [first]
+        for (digit, _), (_, _, radix) in zip(places, stages):
             sizes.append(sizes[-1] // radix)
-            starts.append(starts[-1] // radix)
             offsets.append(pl.multiple_of(offsets[-1] + digit * sizes[-1], 16))
-        return sizes, starts, offsets
-
-    def rs_start(chunk, stage):
-        sizes, starts, offsets = shape_of(chunk)
-        size, radix = sizes[stage + 1], plan.stages[stage][2]
-        for step in range(1, radix):
-            part = lax.rem(digits[stage] + step, radix)
-            copy = remote(
-                pool.at[pl.ds(pl.multiple_of(offsets[stage] + part * size, 16), size)],
-                recv_bufs[stage].at[step - 1, pl.ds(starts[stage + 1], size)],
-                rs_send.at[chunk, stage, step - 1], rs_recv.at[chunk, stage, step - 1],
-                peers[stage][step - 1],
-            )
-            copy.start()
-            later_sends.append(copy)
-
-    def rs_finish(chunk, stage):
-        sizes, starts, offsets = shape_of(chunk)
-        size, radix = sizes[stage + 1], plan.stages[stage][2]
-        for step in range(1, radix):
-            slot = recv_bufs[stage].at[step - 1, pl.ds(starts[stage + 1], size)]
-            remote(
-                slot, slot, rs_send.at[chunk, stage, step - 1], rs_recv.at[chunk, stage, step - 1],
-                peers[stage][step - 1],
-            ).wait_recv()
-        block = row_block(size)
-        target = summed if stage + 1 == len(plan.stages) else pool
-
-        def add(at, carry):
-            own = pl.ds(pl.multiple_of(offsets[stage + 1] + at * block, 16), block)
-            landed = pl.ds(pl.multiple_of(starts[stage + 1] + at * block, 16), block)
-            total = pool[own, :].astype(F32)
+
+        def part(ref, stage, digit):
+            size = sizes[stage + 1]
+            return ref.at[pl.ds(pl.multiple_of(offsets[stage] + digit * size, 16), size)]
+
+        for stage, (_, _, radix) in enumerate(stages):
+            digit, others = places[stage]
+            size, landing = sizes[stage + 1], plan.landing[chunk][stage]
+            sem = rs_recv.at[chunk * plan.most_stages + stage]
             for step in range(1, radix):
-                total = total + recv_bufs[stage][step - 1, landed, :].astype(F32)
-            target[own, :] = total.astype(BF16)
-            return carry
-
-        lax.fori_loop(0, size // block, add, 0)
-
-    def ag_start(chunk, stage):
-        sizes, starts, offsets = shape_of(chunk)
-        part = summed.at[pl.ds(offsets[stage + 1], sizes[stage + 1])]
-        for step in range(1, plan.stages[stage][2]):
-            copy = remote(
-                part, part, ag_send.at[chunk, stage, step - 1], ag_recv.at[chunk, stage, step - 1],
-                peers[stage][step - 1],
-            )
-            copy.start()
-            later_sends.append(copy)
-
-    def ag_finish(chunk, stage):
-        sizes, starts, offsets = shape_of(chunk)
-        size, radix = sizes[stage + 1], plan.stages[stage][2]
-        for step in range(1, radix):
-            sender = lax.rem(digits[stage] + radix - step, radix)
-            part = summed.at[pl.ds(pl.multiple_of(offsets[stage] + sender * size, 16), size)]
-            remote(
-                part, part, ag_send.at[chunk, stage, step - 1], ag_recv.at[chunk, stage, step - 1],
-                peers[stage][step - 1],
-            ).wait_recv()
-
-    pool_copies = []
-
-    def pool_done(chunk):
-        first, last = plan.chunks[chunk]
-        copy = pltpu.make_async_copy(
-            summed.at[pl.ds(first, last - first)], pool_out.at[pl.ds(first, last - first)], out_sem.at[chunk]
-        )
+                remote(
+                    part(pool, stage, lax.rem(digit + step, radix)),
+                    recv.at[pl.ds(landing + (step - 1) * size, size)],
+                    pool_send.at[0], sem, others[step - 1],
+                ).start()
+            yield
+            landed = recv.at[pl.ds(landing, (radix - 1) * size)]
+            remote(landed, landed, pool_send.at[0], sem, others[0]).wait_recv()
+            target = summed if stage + 1 == len(stages) else pool
+            block = row_block(size)
+
+            def add(at, carry):
+                own = pl.ds(pl.multiple_of(offsets[stage + 1] + at * block, 16), block)
+                total = pool[own, :].astype(F32)
+                for step in range(radix - 1):
+                    from_row = pl.multiple_of(landing + step * size + at * block, 16)
+                    total = total + recv[pl.ds(from_row, block), :].astype(F32)
+                target[own, :] = total.astype(BF16)
+                return carry
+
+            lax.fori_loop(0, size // block, add, 0)
+        for stage in reversed(range(len(stages))):
+            radix = stages[stage][2]
+            digit, others = places[stage]
+            size = sizes[stage + 1]
+            sem = ag_recv.at[chunk * plan.most_stages + stage]
+            own = part(summed, stage, digit)
+            for step in range(1, radix):
+                remote(own, own, pool_send.at[1], sem, others[step - 1]).start()
+            yield
+            arriving = summed.at[pl.ds(first, (radix - 1) * size)]
+            remote(arriving, arriving, pool_send.at[1], sem, others[0]).wait_recv()
+        whole = pl.ds(first, last - first)
+        copy = pltpu.make_async_copy(summed.at[whole], pool_out.at[whole], out_sem.at[chunk])
         copy.start()
         pool_copies.append(copy)
 
-    def chunk_events(chunk):
-        if plan.chunks[chunk][0] == plan.chunks[chunk][1]:
-            return
-        count = len(plan.stages)
-        for stage in range(count):
-            rs_start(chunk, stage)
+    def sum_vectors():
+        total, slot = None, 0
+        for at, stage in enumerate(plan.vec_stages):
+            digit, others = place(stage)
+            count = stage[2] - 1
+            for step in range(count):
+                source = vsum.at[other] if at == 0 else vtotal.at[at - 1]
+                remote(
+                    source, vrecv.at[slot + step], vec_send.at[0], vec_recv.at[at], others[step]
+                ).start()
             yield
-            rs_finish(chunk, stage)
-        for stage in reversed(range(count)):
-            ag_start(chunk, stage)
-            yield
-            ag_finish(chunk, stage)
-        pool_done(chunk)
-
-    def vector_events(block):
-        for stage, (_, _, radix) in enumerate(plan.stages):
-            for step in range(1, radix):
-                copy = remote(
-                    vsum.at[block, stage], vrecv.at[block, stage, step - 1],
-                    vec_send.at[block, stage, step - 1], vec_recv.at[block, stage, step - 1],
-                    peers[stage][step - 1],
-                )
-                copy.start()
-                later_sends.append(copy)
-            yield
-            total = vsum[block, stage]
-            for step in range(1, radix):
-                slot = vrecv.at[block, stage, step - 1]
-                remote(
-                    slot, slot, vec_send.at[block, stage, step - 1],
-                    vec_recv.at[block, stage, step - 1], peers[stage][step - 1],
-                ).wait_recv()
-                total = total + vrecv[block, stage, step - 1]
-            vsum[block, stage + 1] = total
-
-    running = []
-
-    def begin(events):
-        if next(events, "done") != "done":
-            running.append(events)
-
-    def tick():
-        for events in list(running):
-            if next(events, "done") == "done":
-                running.remove(events)
+            landed = vrecv.at[pl.ds(slot, count)]
+            remote(landed, landed, vec_send.at[0], vec_recv.at[at], others[0]).wait_recv()
+            total = vsum[sec] if at == 0 else vtotal[at - 1]
+            for step in range(count):
+                total = total + vrecv[slot + step]
+            vtotal[at] = total
+            slot += count
+
+    def tick(which):
+        if which not in running:
+            running[which] = sum_vectors() if which == VECTORS else sum_chunk(which)
+        if running[which] is not None and next(running[which], "done") == "done":
+            running[which] = None
+
+    def run(steps):
+        for step in steps:
+            if isinstance(step, int):
+                if step == VECTORS or plan.chunks[step][0] < plan.chunks[step][1]:
+                    tick(step)
+            else:
+                step[0](*step[1:])
+
+    results = []
+
+    def send_result(at):
+        value, result = ((outv, blocks_out), (gin, grads_out))[at]
+        for row in range(half):
+            rows = pl.ds(row * length, length)
+            target = result.at[0, sec * half + row]
+            landing = result.at[0, other * half + row]
+            local = pltpu.make_async_copy(value.at[sec, rows], target, out_send.at[0, at, row])
+            sems = out_send.at[1, at, row], out_recv.at[at, row]
+            away = remote(value.at[other, rows], target, *sems, other_core)
+            local.start()
+            away.start()
+            results.append((local, away, remote(value.at[other, rows], landing, *sems, other_core)))
 
     wait_block(0)
     build_masks()
@@ -547,53 +549,19 @@
     loads[5].wait()
     forward_in(1)
     forward_out(1)
-    up_weight_grad(1)
-    begin(chunk_events(0))
-    backward_out(1)
-    tick()
-    kernel_grad(1)
-    begin(chunk_events(1))
-    tick()
-    backward_in(1)
-    tick()
-    down_weight_grad(1)
-    up_weight_grad(0)
-    begin(chunk_events(2))
-    begin(vector_events(1))
-    tick()
-    backward_out(0)
-    tick()
-    kernel_grad(0)
-    begin(chunk_events(3))
-    tick()
-    backward_in(0)
-    tick()
-    down_weight_grad(0)
+    send_result(0)
     if plan.pool_rows > plan.used_rows:
         pool[plan.used_rows : plan.pool_rows, :] = jnp.zeros(
             (plan.pool_rows - plan.used_rows, 128), BF16
         )
-    begin(chunk_events(4))
-    begin(vector_events(0))
-
-    copies = []
-    for at, (value, result) in enumerate(((outv, blocks_out), (gin, grads_out))):
-        for row in range(half):
-            rows = pl.ds(row * length, length)
-            target = result.at[0, sec * half + row]
-            landing = result.at[0, other * half + row]
-            copies.append((
-                pltpu.make_async_copy(value.at[sec, rows], target, out_send.at[0, at, row]),
-                remote(value.at[other, rows], target, out_send.at[1, at, row], out_recv.at[at, row], other_core),
-                remote(value.at[other, rows], landing, out_send.at[1, at, row], out_recv.at[at, row], other_core),
-            ))
-    for local, away, _ in copies:
-        local.start()
-        away.start()
-    while running:
-        tick()
-    vec_out[...] = vsum[sec, len(plan.stages)]
-    for local, away, arrives in copies:
+    run((
+        (up_weight_grad, 1), (backward_out, 1), 0, (kernel_grad, 1, 1), (kernel_grad, 1, 0), (kernel_grad, 1, 2), 0, 1, (backward_mid, 1), 1, (down_weight_grad, 1), (backward_in, 1), 0, (up_weight_grad, 0), 2, 3, 1, (backward_out, 0), 0, 3, (kernel_grad, 0, 0), (kernel_grad, 0, 1), 2, 1, (kernel_grad, 0, 3), (kernel_grad, 0, 4), (kernel_grad, 0, 2), 5, 0, 3, (backward_mid, 0), 4, 5, 1, 2, 4, 3, 2, 5, (down_weight_grad, 0), 0, 1, 6, 3, 4, 5, 6, 2, 4, 1, 5, 2, 3, 6, 1, 0, 4, 5, 2, 6, 3, 1, 5, 4, 2, 6, (backward_in, 0), (send_result, 1), VECTORS, 4, 5, 5, 2, 3, 6, 4, 6, 3, 4,
+    ))
+
+    while any(events is not None for events in running.values()):
+        run(tuple(range(len(plan.chunks))) + (VECTORS,))
+    vec_out[...] = vtotal[len(plan.vec_stages) - 1]
+    for local, away, arrives in results:
         local.wait()
         away.wait_send()
         arrives.wait_recv()
@@ -601,22 +569,30 @@
         copy.wait()
     for copy in later_sends:
         copy.wait_send()
+    for at in range(2):
+        everything = summed.at[pl.ds(0, plan.sent_rows)]
+        remote(everything, everything, pool_send.at[at], rs_recv.at[0], other_core).wait_send()
+    remote(vrecv, vrecv, vec_send.at[0], vec_recv.at[0], other_core).wait_send()
 
 
 def final_kernel(plan, blocks_in, grads_in, pool_in, vec, *refs):
     (
         blocks_out, grads_out, g_in_gain, g_in_shift, g_down, g_down_bias, g_mid_gain, g_mid_shift,
         g_enc, g_dec, g_conv_bias, g_out_gain, g_out_shift, g_up, g_up_bias,
-        up_pool, down_pool, tap_pool, up_full, down_full, enc_full, dec_full,
+        bounce, up_pool, down_pool, tap_pool, up_full, down_full, enc_full, dec_full,
         in_sem, out_sem,
     ) = refs
     sec = lax.axis_index("section")
     width, inner = plan.width, plan.inner
+    entering = [
+        pltpu.make_async_copy(blocks_in, bounce.at[0], in_sem.at[4]),
+        pltpu.make_async_copy(grads_in, bounce.at[1], in_sem.at[5]),
+    ]
     passed = [
-        pltpu.make_async_copy(blocks_in, blocks_out, out_sem.at[0]),
-        pltpu.make_async_copy(grads_in, grads_out, out_sem.at[1]),
+        pltpu.make_async_copy(bounce.at[0], blocks_out, out_sem.at[0]),
+        pltpu.make_async_copy(bounce.at[1], grads_out, out_sem.at[1]),
     ]
-    for copy in passed:
+    for copy in entering:
         copy.start()
 
     def load(name, target, size, sem):
@@ -656,12 +632,15 @@
         left = rest_of(ref, main * rows, rest, tiles)
         full[:, main * 128 :] = left.T[:rows, :]
 
+    for first, second in zip(entering, passed):
+        first.wait()
+        second.start()
     up_load.wait()
     unpack(up_pool, up_full, inner, plan.up_main, plan.up_rest, plan.in_tiles)
     up_store = pltpu.make_async_copy(up_full, g_up.at[0], out_sem.at[2])
     up_store.start()
     down_load.wait()
-    unpack(down_pool, down_full, width, plan.in_main, plan.in_rest, plan.width_tiles)
+    unpack(down_pool, down_full, inner, plan.up_main, plan.up_rest, plan.in_tiles)
     down_store = pltpu.make_async_copy(down_full, g_down.at[0], out_sem.at[3])
     down_store.start()
     part = inner // 2
@@ -693,9 +672,8 @@
         block_inputs, cotangent, segment_ids, in_gain, in_shift, down_weight, down_bias, mid_gain,
         mid_shift, enc_kernel, dec_kernel, conv_bias, out_gain, out_shift, up_weight, up_bias,
     ) = args
+    args = args[:5] + (jnp.swapaxes(down_weight, 1, 2),) + args[6:]
     length, width, inner, half, tokens = plan.length, plan.width, plan.inner, plan.half, plan.tokens
-    stages = len(plan.stages)
-    most = max(radix for _, _, radix in plan.stages) - 1
     chunks = len(plan.chunks)
     any_spec = pl.BlockSpec(memory_space=pl.ANY)
     vmem_spec = pl.BlockSpec(memory_space=pltpu.VMEM)
@@ -703,10 +681,6 @@
     narrow = lambda kind: pltpu.VMEM((2, tokens, inner), kind)
     factor = pltpu.VMEM((2, tokens, 128), F32)
     dma = pltpu.SemaphoreType.DMA
-    recv_bufs, left = [], plan.pool_rows
-    for _, _, radix in plan.stages:
-        left //= radix
-        recv_bufs.append(pltpu.VMEM((radix - 1, left, 128), BF16))
     enc_taps, dec_taps = plan.taps
     blocks, grads, pool, vectors = pl.pallas_call(
         functools.partial(main_kernel, plan),
@@ -722,7 +696,7 @@
         scratch_shapes=[
             pltpu.VMEM((2, half, length, width), BF16),
             pltpu.VMEM((half, length, width), BF16),
-            pltpu.VMEM((2, width, inner), BF16),
+            pltpu.VMEM((2, inner, width), BF16),
             pltpu.VMEM((2, inner, width), BF16),
             pltpu.VMEM((enc_taps, inner, inner), BF16),
             pltpu.VMEM((dec_taps, inner, inner), BF16),
@@ -742,15 +716,16 @@
             wide(BF16),
             pltpu.VMEM((plan.pool_rows, 128), BF16),
             pltpu.VMEM((plan.pool_rows, 128), BF16),
-            pltpu.VMEM((2, stages + 1, 16, 512), F32),
-            pltpu.VMEM((2, stages, most, 16, 512), F32),
+            pltpu.VMEM((plan.recv_rows, 128), BF16),
+            pltpu.VMEM((2, 16, 512), F32),
+            pltpu.VMEM((len(plan.vec_stages), 16, 512), F32),
+            pltpu.VMEM((plan.vec_copies, 16, 512), F32),
             dma((6,)), dma((4,)), dma((4,)), dma((2,)), dma((2,)),
             dma((2, 2, half, 2)), dma((2, 2, half, 2)),
-            dma((chunks, stages, most)), dma((chunks, stages, most)),
-            dma((chunks, stages, most)), dma((chunks, stages, most)),
-            dma((2, stages, most)), dma((2, stages, most)),
+            dma((2,)), dma((chunks * plan.most_stages,)), dma((chunks * plan.most_stages,)),
+            dma((1,)), dma((len(plan.vec_stages),)),
             dma((chunks,)), dma((2, 2, half)), dma((2, half)),
-        ] + recv_bufs,
+        ],
         compiler_params=pltpu.CompilerParams(
             collective_id=0, has_side_effects=True, vmem_limit_bytes=VMEM_LIMIT
         ),
@@ -758,13 +733,13 @@
     )(*args)
     vector = lambda size: jax.ShapeDtypeStruct((1, size), F32)
     part = inner // 2
-    return pl.pallas_call(
+    results = pl.pallas_call(
         functools.partial(final_kernel, plan),
         out_shape=(
             jax.ShapeDtypeStruct(block_inputs.shape, BF16),
             jax.ShapeDtypeStruct(block_inputs.shape, BF16),
             vector(width), vector(width),
-            jax.ShapeDtypeStruct((1, width, inner), F32),
+            jax.ShapeDtypeStruct((1, inner, width), F32),
             vector(inner), vector(inner), vector(inner),
             jax.ShapeDtypeStruct((enc_taps, inner, part), F32),
             jax.ShapeDtypeStruct((dec_taps, inner, part), F32),
@@ -776,18 +751,20 @@
         out_specs=(any_spec, any_spec, vmem_spec, vmem_spec, any_spec, vmem_spec, vmem_spec, vmem_spec,
                    any_spec, any_spec, vmem_spec, vmem_spec, vmem_spec, any_spec, vmem_spec),
         scratch_shapes=[
+            pltpu.VMEM((2,) + block_inputs.shape, BF16),
             pltpu.VMEM((plan.up_rows, 128), BF16),
             pltpu.VMEM((plan.down_rows, 128), BF16),
             pltpu.VMEM((plan.tap_rows * (enc_taps + dec_taps), 128), BF16),
             pltpu.VMEM((inner, width), F32),
-            pltpu.VMEM((width, inner), F32),
+            pltpu.VMEM((inner, width), F32),
             pltpu.VMEM((enc_taps, inner, part), F32),
             pltpu.VMEM((dec_taps, inner, part), F32),
-            dma((4,)), dma((6,)),
+            dma((6,)), dma((6,)),
         ],
         compiler_params=pltpu.CompilerParams(vmem_limit_bytes=VMEM_LIMIT),
         name="unpack_sums",
     )(blocks, grads, pool, vectors)
+    return results[:4] + (jnp.swapaxes(results[4], 1, 2),) + results[5:]
 
 
 def solution(mesh):

time: 198 us -> 103 us (0.52)
  Pallas kernels: 191 us -> 102 us
  local copies, waits for them, and re-layouts: 5.32 us -> 0 us
    pallas_call x1, Pallas kernels: 86 us -> 7.94 us  [per_device(): pl.pallas_call(functools.partial(final_kernel, plan), out_shape=(jax.Shap...]
    pallas_call x1, Pallas kernels: 105 us -> 94.2 us  [per_device(): pl.pallas_call(functools.partial(main_kernel, plan), out_shape=(jax.Shape...]
    pallas_call x1 -> x0, local copies, waits for them, and re-layouts: 3.04 us -> none  [per_device(): pl.pallas_call(functools.partial(final_kernel, plan), out_shape=(jax.Shap...]
    unnamed x1 -> x0, local copies, waits for them, and re-layouts: 2.28 us -> none
where the time goes in v2:
time: 103 us
  Pallas kernels  102 us (99%)
    pallas_call x1, Pallas kernels, per_device(): pl.pallas_call(functools.partial(main_kernel, plan), out_shape=(jax.Shape...  94.2 us
    pallas_call x1, Pallas kernels, per_device(): pl.pallas_call(functools.partial(final_kernel, plan), out_shape=(jax.Shap...  7.94 us

profile of v2, /device:TPU:0, one launch (start us, length us, event | category | flops | bytes accessed | tf_op | source)
XLA Modules:
  0.0 102.8 jit_solution(17256236977400291707)
XLA Ops:
  0.7 94.2 %blocks_and_sums.1 = (bf16[1,4,192,800]{3,2,1,0:T(8,128)(2,1)}, bf16[1,4,192,800]{3,2,1,0:T(8,128)(2,1)}, bf16[20480,128]{1,0:T(8,128)(2,1)}, f32[16,512]{1,0:T(8,128)}) custom-call(bf16[1,4,192,800]{3,2,1,0:T(8,128)(2,1)} %refs_0_.1, bf16[4,192,800]{2,1,0:T(8,128)(2,1)} %refs_1_.1, s32[4,192]{1,0:T(4,128)} %refs_2_.1, f32[1,800]{1,0:T(1,128)} %refs_3_.1, ...), custom_call_target="tpu_custom_call" | custom-call | tf_op jit(solution)/shard_map/blocks_and_sums/pallas_call | solution.py:685
  94.9 7.9 %unpack_sums.1 = (bf16[1,4,192,800]{3,2,1,0:T(8,128)(2,1)}, bf16[1,4,192,800]{3,2,1,0:T(8,128)(2,1)}, f32[1,800]{1,0:T(1,128)}, f32[1,800]{1,0:T(1,128)}, f32[1,...) custom-call(bf16[1,4,192,800]{3,2,1,0:T(8,128)(2,1)} %get-tuple-elem, ...), custom_call_target="tpu_custom_call" | custom-call | tf_op jit(solution)/shard_map/unpack_sums/pallas_call | solution.py:736

commit v3 on v2

--- a/solution.py
+++ b/solution.py
@@ -67,7 +67,8 @@
     return best
 
 
-CHUNKS = ((('up', 1, 0), 'direct'), (('kernel', 1, 9), 'std'), (('down', 1, 0), 'std'), (('up', 0, 0), 'std'), (('kernel', 0, 2), 'std'), (('kernel', 0, 9), 'std'), (('down', 0, 0), 'direct'))
+PARTS = 40
+CHUNKS = ((7, 'std'), (11, 'std'), (17, 'std'), (24, 'std'), (26, 'std'), (32, 'std'), (34, 'std'), (40, 'std'))
 
 
 class Plan:
@@ -86,15 +87,13 @@
         self.down_rows = self.up_rows
         self.tap_rows = self.in_main * inner + self.in_rest * self.in_tiles
         position = 0
-        self.at, ends = {}, {}
+        self.at = {}
         for name, block, size, pieces in (
             ("up", 1, self.up_rows, 1), ("kernel", 1, self.tap_rows, dec_taps), ("down", 1, self.down_rows, 1),
             ("up", 0, self.up_rows, 1), ("kernel", 0, self.tap_rows, enc_taps), ("down", 0, self.down_rows, 1),
         ):
             self.at[name, block] = position
-            for piece in range(pieces):
-                position += size
-                ends[name, block, piece] = position
+            position += size * pieces
         self.used_rows = position
         section = [("section", (1, 1), 2)]
         bits = self.n_seq.bit_length() - 1
@@ -111,13 +110,13 @@
                   "direct": section + direct + layers}
         self.vec_stages = orders["direct"]
         unit = 32 * self.n_seq * self.n_dp
+        self.pool_rows = -(-self.used_rows // unit) * unit
+        nominal = -(-self.used_rows // 512) * 512
         self.chunks, first = [], 0
-        for (name, block, piece), order in CHUNKS:
-            last = ends[name, block, min(piece, self.taps[block] - 1)]
-            last = -(-last // unit) * unit if last == self.used_rows else last // unit * unit
+        for end, order in CHUNKS:
+            last = self.pool_rows if end == PARTS else nominal * end // PARTS // unit * unit
             self.chunks.append((first, last, orders[order]))
             first = last
-        self.pool_rows = first
         self.landing, self.recv_rows = [], 0
         for first, last, stages in self.chunks:
             size, places = last - first, []
@@ -137,7 +136,7 @@
         enc_in, dec_in, conv_bias, out_gain, out_shift, up_in, up_bias,
         blocks_out, grads_out, pool_out, vec_out,
         xin, cot, wd, wu, ek, dk, vec, seg_side, masks,
-        n1, s1, q1, n2, s2, q2, n3, s3, q3, fa, mid, win, la, outv, cp, hp, gin,
+        n1, s1, q1, n2, s2, q2, n3, s3, q3, fa, mid, win, la, outv, cp, hp, gin, dl,
         pool, summed, recv, vsum, vtotal, vrecv,
         load_sem, pair_send, pair_recv, seg_send, seg_recv, halo_send, halo_recv,
         pool_send, rs_recv, ag_recv, vec_send, vec_recv, out_sem, out_send, out_recv,
@@ -166,7 +165,7 @@
         pltpu.make_async_copy(up_in.at[0], wu.at[sec], load_sem.at[2]),
         pltpu.make_async_copy(enc_in, ek, load_sem.at[3]),
         pltpu.make_async_copy(dec_in, dk, load_sem.at[4]),
-        pltpu.make_async_copy(cot_in.at[own_rows], cot, load_sem.at[5]),
+        pltpu.make_async_copy(cot_in.at[own_rows], cot.at[0], load_sem.at[5]),
     ]
     for load in loads:
         load.start()
@@ -234,108 +233,110 @@
         for copy in seg_copies:
             copy.wait_recv()
         ext = plan.ext
-        place = lax.broadcasted_iota(jnp.int32, (ext, length), 0)
+        position = lax.broadcasted_iota(jnp.int32, (ext, length), 0)
         token = lax.broadcasted_iota(jnp.int32, (ext, length), 1)
         for row in range(half):
             at = pl.ds(sec * half + row, 1)
             own = (seg_in[at, :] + 1).astype(F32)
             before = jnp.where(seq > 0, (seg_side[0, at, :] + 1).astype(F32), 0.0)
             after = jnp.where(seq < plan.n_seq - 1, (seg_side[1, at, :] + 1).astype(F32), 0.0)
-            spread = jnp.where(place - MARGIN == token, own, 0.0)
-            spread = spread + jnp.where(place + (length - MARGIN) == token, before, 0.0)
-            spread = spread + jnp.where(place - (length + MARGIN) == token, after, 0.0)
-            numbers = dot(spread.astype(BF16), jnp.ones((length, 128), BF16), 1, 0)
+            numbers = jnp.where(position - MARGIN == token, own, 0.0)
+            numbers = numbers + jnp.where(position + (length - MARGIN) == token, before, 0.0)
+            numbers = numbers + jnp.where(position - (length + MARGIN) == token, after, 0.0)
+            numbers = dot(numbers.astype(BF16), jnp.ones((length, 128), BF16), 1, 0)
             here = numbers[MARGIN : MARGIN + length]
             for at_offset, offset in enumerate(OFFSETS):
                 there = numbers[MARGIN + offset : MARGIN + offset + length]
                 masks[at_offset, row] = jnp.where(there == here, 1.0, 0.0).astype(BF16)
 
-    def window(ext_ref, block, row, offset):
-        piece = ext_ref[block, row, MARGIN + offset : MARGIN + offset + length, :]
+    edges = [span for row in range(half) for span in ((row, 0, MARGIN), (row, length - MARGIN, length))]
+    middle = [(row, MARGIN, length - MARGIN) for row in range(half)]
+    everywhere = [(row, 0, length) for row in range(half)]
+
+    def take(ref, at, part, offset=0):
+        return jnp.concatenate(
+            [ref[at, row, low + offset : high + offset, :] for row, low, high in part], axis=0
+        )
+
+    def put(ref, at, part, value, offset=0):
+        done = 0
+        for row, low, high in part:
+            ref[at, row, low + offset : high + offset, :] = value[done : done + high - low]
+            done += high - low
+
+    def window(ref, block, offset):
+        piece = take(ref, block, everywhere, MARGIN + offset)
         if offset == 0:
             return piece
-        return piece * across(masks[OFFSETS.index(offset), row], inner)
+        return piece * across(take(masks, OFFSETS.index(offset), everywhere), inner)
 
     def params(block):
         wide = [vec[block, at : at + 1, :] for at in range(3)]
         narrow = [vec[block, 3 + at : 4 + at, :inner] for at in range(6)]
         return wide + narrow
 
-    def token_rows(row):
-        return pl.ds(pl.multiple_of(row * length, length), length)
-
-    def halo(ref, which, block, row):
+    def halo(ref, which, block):
         copies = []
-        if block == 0 or which == 0:
-            copies.append(remote(
-                ref.at[block, row, pl.ds(length, MARGIN)], ref.at[block, row, pl.ds(0, MARGIN)],
-                halo_send.at[which, block, row, 0], halo_recv.at[which, block, row, 0], right,
-            ))
-        if block == 0 or which == 1:
-            copies.append(remote(
-                ref.at[block, row, pl.ds(MARGIN, MARGIN)], ref.at[block, row, pl.ds(length + MARGIN, MARGIN)],
-                halo_send.at[which, block, row, 1], halo_recv.at[which, block, row, 1], left,
-            ))
+        for row in range(half):
+            if block == 0 or which == 0:
+                copies.append(remote(
+                    ref.at[block, row, pl.ds(length, MARGIN)], ref.at[block, row, pl.ds(0, MARGIN)],
+                    halo_send.at[which, block, row, 0], halo_recv.at[which, block, row, 0], right,
+                ))
+            if block == 0 or which == 1:
+                copies.append(remote(
+                    ref.at[block, row, pl.ds(MARGIN, MARGIN)],
+                    ref.at[block, row, pl.ds(length + MARGIN, MARGIN)],
+                    halo_send.at[which, block, row, 1], halo_recv.at[which, block, row, 1], left,
+                ))
         return copies
 
-    def each_row(body):
-        def step(row, carry):
-            body(row)
-            return carry
-
-        lax.fori_loop(0, half, step, 0)
-
-    def entry(block, row):
-        values = xin[block, row].astype(F32)
+    def entry(block, part):
+        values = take(xin, block, part).astype(F32)
         if block == 1:
-            values = values + outv[0, token_rows(row)].astype(F32)
+            values = values + take(outv, 0, part).astype(F32)
         return values
+
+    def spread(factor):
+        return jnp.broadcast_to(factor, (factor.shape[0], 128))
 
     def forward_in(block):
         p = params(block)
-
-        def body(row):
-            at = token_rows(row)
-            normed, factor, act, slope = norm_act(entry(block, row), p[0], p[1])
-            n1[block, at] = normed
-            s1[block, at] = slope
-            q1[block, at] = jnp.broadcast_to(factor, (length, 128))
+        for part in (edges, middle):
+            normed, factor, act, slope = norm_act(entry(block, part), p[0], p[1])
+            put(n1, block, part, normed)
+            put(s1, block, part, slope)
+            put(q1, block, part, spread(factor))
             act = act.astype(BF16)
-            fa[block, at] = act
+            put(fa, block, part, act)
             hidden = dot(act, wd[block], 1, 1) + p[3]
             normed, factor, act, slope = norm_act(hidden, p[4], p[5])
-            n2[block, at] = normed
-            s2[block, at] = slope
-            q2[block, at] = jnp.broadcast_to(factor, (length, 128))
-            mid[block, row, MARGIN : MARGIN + length, :] = act.astype(BF16)
-            for copy in halo(mid, 0, block, row):
-                copy.start()
-
-        each_row(body)
+            put(n2, block, part, normed)
+            put(s2, block, part, slope)
+            put(q2, block, part, spread(factor))
+            put(mid, block, part, act.astype(BF16), MARGIN)
+            if part is edges:
+                for copy in halo(mid, 0, block):
+                    copy.start()
 
     def forward_out(block):
         p = params(block)
-
-        def body(row):
-            at = token_rows(row)
-            for copy in halo(mid, 0, block, row):
-                copy.wait()
-            total = None
-            for tap in range(plan.taps[block]):
-                piece = window(mid, block, row, (tap - 2) * DILATION)
-                win[block, tap, at] = piece
-                term = dot(piece, kernels[block][tap], 1, 0)
-                total = term if total is None else total + term
-            normed, factor, act, slope = norm_act(total + p[6], p[7], p[8])
-            n3[block, at] = normed
-            s3[block, at] = slope
-            q3[block, at] = jnp.broadcast_to(factor, (length, 128))
-            act = act.astype(BF16)
-            la[block, at] = act
-            result = entry(block, row) + dot(act, wu[block], 1, 0) + p[2]
-            outv[block, at] = result.astype(BF16)
-
-        each_row(body)
+        for copy in halo(mid, 0, block):
+            copy.wait()
+        total = None
+        for tap in range(plan.taps[block]):
+            piece = window(mid, block, (tap - 2) * DILATION)
+            put(win, block * plan.taps[0] + tap, everywhere, piece)
+            term = dot(piece, kernels[block][tap], 1, 0)
+            total = term if total is None else total + term
+        normed, factor, act, slope = norm_act(total + p[6], p[7], p[8])
+        put(n3, block, everywhere, normed)
+        put(s3, block, everywhere, slope)
+        put(q3, block, everywhere, spread(factor))
+        act = act.astype(BF16)
+        put(la, block, everywhere, act)
+        result = entry(block, everywhere) + dot(act, wu[block], 1, 0) + p[2]
+        put(outv, block, everywhere, result.astype(BF16))
 
     def add_wide(block, at, value):
         vsum[block, at : at + 1, :] += value[:, :512]
@@ -344,65 +345,63 @@
     def add_narrow(block, at, value):
         vsum[block, at : at + 1, :inner] += value
 
-    def upstream_of(block, row):
-        return cot[row] if block == 1 else gin[1, token_rows(row)]
+    def upstream_of(block, part):
+        return take(cot, 0, part) if block == 1 else take(gin, 1, part)
+
+    def last_grad(block):
+        incoming = upstream_of(block, everywhere)
+        add_wide(block, 4, jnp.sum(incoming.astype(F32), axis=0, keepdims=True))
+        put(dl, 0, everywhere, dot(incoming, wu[block], 1, 1))
 
     def backward_out(block):
         p = params(block)
-
-        def body(row):
-            at = token_rows(row)
-            incoming = upstream_of(block, row)
-            add_wide(block, 4, jnp.sum(incoming.astype(F32), axis=0, keepdims=True))
-            d_last = dot(incoming, wu[block], 1, 1)
+        for part in (edges, middle):
+            if block == 1:
+                d_last = take(dl, 0, part)
+            else:
+                incoming = upstream_of(block, part)
+                add_wide(block, 4, jnp.sum(incoming.astype(F32), axis=0, keepdims=True))
+                d_last = dot(incoming, wu[block], 1, 1)
             d_conv, gain_grad, shift_grad = norm_act_back(
-                d_last, s3[block, at], n3[block, at], across(q3[block, at], inner), p[7]
+                d_last, take(s3, block, part), take(n3, block, part),
+                across(take(q3, block, part), inner), p[7],
             )
             add_narrow(block, 10, gain_grad)
             add_narrow(block, 11, shift_grad)
             add_narrow(block, 9, jnp.sum(d_conv, axis=0, keepdims=True))
-            cp[block, row, MARGIN : MARGIN + length, :] = d_conv.astype(BF16)
-            for copy in halo(cp, 1, block, row):
-                copy.start()
-
-        each_row(body)
+            put(cp, block, part, d_conv.astype(BF16), MARGIN)
+            if part is edges:
+                for copy in halo(cp, 1, block):
+                    copy.start()
 
     def backward_mid(block):
         p = params(block)
-
-        def body(row):
-            at = token_rows(row)
-            for copy in halo(cp, 1, block, row):
-                copy.wait()
-            total = None
-            for tap in range(plan.taps[block]):
-                piece = window(cp, block, row, -(tap - 2) * DILATION)
-                term = dot(piece, kernels[block][tap], 1, 1)
-                total = term if total is None else total + term
-            d_hidden, gain_grad, shift_grad = norm_act_back(
-                total, s2[block, at], n2[block, at], across(q2[block, at], inner), p[4]
-            )
-            add_narrow(block, 7, gain_grad)
-            add_narrow(block, 8, shift_grad)
-            add_narrow(block, 6, jnp.sum(d_hidden, axis=0, keepdims=True))
-            hp[block, at] = d_hidden.astype(BF16)
-
-        each_row(body)
+        for copy in halo(cp, 1, block):
+            copy.wait()
+        total = None
+        for tap in range(plan.taps[block]):
+            term = dot(window(cp, block, -(tap - 2) * DILATION), kernels[block][tap], 1, 1)
+            total = term if total is None else total + term
+        d_hidden, gain_grad, shift_grad = norm_act_back(
+            total, take(s2, block, everywhere), take(n2, block, everywhere),
+            across(take(q2, block, everywhere), inner), p[4],
+        )
+        add_narrow(block, 7, gain_grad)
+        add_narrow(block, 8, shift_grad)
+        add_narrow(block, 6, jnp.sum(d_hidden, axis=0, keepdims=True))
+        put(hp, block, everywhere, d_hidden.astype(BF16))
 
     def backward_in(block):
         p = params(block)
-
-        def body(row):
-            at = token_rows(row)
-            d_first = dot(hp[block, at], wd[block], 1, 0)
-            d_entry, gain_grad, shift_grad = norm_act_back(
-                d_first, s1[block, at], n1[block, at], across(q1[block, at], width), p[0]
-            )
-            add_wide(block, 0, gain_grad)
-            add_wide(block, 2, shift_grad)
-            gin[block, at] = (upstream_of(block, row).astype(F32) + d_entry).astype(BF16)
-
-        each_row(body)
+        d_first = dot(take(hp, block, everywhere), wd[block], 1, 0)
+        d_entry, gain_grad, shift_grad = norm_act_back(
+            d_first, take(s1, block, everywhere), take(n1, block, everywhere),
+            across(take(q1, block, everywhere), width), p[0],
+        )
+        add_wide(block, 0, gain_grad)
+        add_wide(block, 2, shift_grad)
+        incoming = upstream_of(block, everywhere).astype(F32)
+        put(gin, block, everywhere, (incoming + d_entry).astype(BF16))
 
     def to_pool(position, left_value, right_value):
         rows, columns = left_value.shape[1], right_value.shape[1]
@@ -420,20 +419,17 @@
                 :, tile * 128 : tile * 128 + lanes
             ]
 
-    def upstream_all(block):
-        return jnp.concatenate([upstream_of(block, row) for row in range(half)], axis=0)
-
     def up_weight_grad(block):
-        to_pool(plan.at["up", block], la[block], upstream_all(block))
+        to_pool(plan.at["up", block], take(la, block, everywhere), upstream_of(block, everywhere))
 
     def kernel_grad(block, tap):
-        grad = jnp.concatenate(
-            [cp[block, row, MARGIN : MARGIN + length, :] for row in range(half)], axis=0
+        to_pool(
+            plan.at["kernel", block] + tap * plan.tap_rows,
+            take(win, block * plan.taps[0] + tap, everywhere), take(cp, block, everywhere, MARGIN),
         )
-        to_pool(plan.at["kernel", block] + tap * plan.tap_rows, win[block, tap], grad)
 
     def down_weight_grad(block):
-        to_pool(plan.at["down", block], hp[block], fa[block])
+        to_pool(plan.at["down", block], take(hp, block, everywhere), take(fa, block, everywhere))
 
     pool_copies, running = [], {}
 
@@ -529,25 +525,25 @@
     def send_result(at):
         value, result = ((outv, blocks_out), (gin, grads_out))[at]
         for row in range(half):
-            rows = pl.ds(row * length, length)
             target = result.at[0, sec * half + row]
             landing = result.at[0, other * half + row]
-            local = pltpu.make_async_copy(value.at[sec, rows], target, out_send.at[0, at, row])
+            local = pltpu.make_async_copy(value.at[sec, row], target, out_send.at[0, at, row])
             sems = out_send.at[1, at, row], out_recv.at[at, row]
-            away = remote(value.at[other, rows], target, *sems, other_core)
+            away = remote(value.at[other, row], target, *sems, other_core)
             local.start()
             away.start()
-            results.append((local, away, remote(value.at[other, rows], landing, *sems, other_core)))
+            results.append((local, away, remote(value.at[other, row], landing, *sems, other_core)))
 
     wait_block(0)
+    forward_in(0)
     build_masks()
-    forward_in(0)
     loads[3].wait()
     forward_out(0)
     wait_block(1)
+    forward_in(1)
+    loads[5].wait()
+    last_grad(1)
     loads[4].wait()
-    loads[5].wait()
-    forward_in(1)
     forward_out(1)
     send_result(0)
     if plan.pool_rows > plan.used_rows:
@@ -555,7 +551,7 @@
             (plan.pool_rows - plan.used_rows, 128), BF16
         )
     run((
-        (up_weight_grad, 1), (backward_out, 1), 0, (kernel_grad, 1, 1), (kernel_grad, 1, 0), (kernel_grad, 1, 2), 0, 1, (backward_mid, 1), 1, (down_weight_grad, 1), (backward_in, 1), 0, (up_weight_grad, 0), 2, 3, 1, (backward_out, 0), 0, 3, (kernel_grad, 0, 0), (kernel_grad, 0, 1), 2, 1, (kernel_grad, 0, 3), (kernel_grad, 0, 4), (kernel_grad, 0, 2), 5, 0, 3, (backward_mid, 0), 4, 5, 1, 2, 4, 3, 2, 5, (down_weight_grad, 0), 0, 1, 6, 3, 4, 5, 6, 2, 4, 1, 5, 2, 3, 6, 1, 0, 4, 5, 2, 6, 3, 1, 5, 4, 2, 6, (backward_in, 0), (send_result, 1), VECTORS, 4, 5, 5, 2, 3, 6, 4, 6, 3, 4,
+        (backward_out, 1), (up_weight_grad, 1), (kernel_grad, 1, 0), 0, (backward_mid, 1), (kernel_grad, 1, 2), 0, (down_weight_grad, 1), (kernel_grad, 1, 1), 2, (backward_in, 1), 2, (backward_out, 0), 0, 1, (kernel_grad, 0, 0), (up_weight_grad, 0), (kernel_grad, 0, 1), 3, 1, (kernel_grad, 0, 2), (kernel_grad, 0, 3), 2, 5, 0, 3, (backward_mid, 0), 2, 1, 5, (down_weight_grad, 0), 0, (kernel_grad, 0, 4), 7, 3, 1, 7, 2, 5, 3, 0, 6, 4, 6, 1, 7, 4, 5, 0, 2, 3, 1, 7, 6, 4, 2, 5, 3, 4, 6, 7, 1, 5, 3, 4, 6, 2, 7, 0, 2, 1, 5, 6, 4, 0, 1, 7, 3, 4, 5, 6, (backward_in, 0), (send_result, 1), VECTORS, 7, 4, 6, 5, 3, 7, 4, 6,
     ))
 
     while any(events is not None for events in running.values()):
@@ -677,9 +673,9 @@
     chunks = len(plan.chunks)
     any_spec = pl.BlockSpec(memory_space=pl.ANY)
     vmem_spec = pl.BlockSpec(memory_space=pltpu.VMEM)
-    wide = lambda kind: pltpu.VMEM((2, tokens, width), kind)
-    narrow = lambda kind: pltpu.VMEM((2, tokens, inner), kind)
-    factor = pltpu.VMEM((2, tokens, 128), F32)
+    wide = lambda kind: pltpu.VMEM((2, half, length, width), kind)
+    narrow = lambda kind: pltpu.VMEM((2, half, length, inner), kind)
+    factor = pltpu.VMEM((2, half, length, 128), F32)
     dma = pltpu.SemaphoreType.DMA
     enc_taps, dec_taps = plan.taps
     blocks, grads, pool, vectors = pl.pallas_call(
@@ -695,7 +691,7 @@
         out_specs=(any_spec, any_spec, any_spec, vmem_spec),
         scratch_shapes=[
             pltpu.VMEM((2, half, length, width), BF16),
-            pltpu.VMEM((half, length, width), BF16),
+            pltpu.VMEM((1, half, length, width), BF16),
             pltpu.VMEM((2, inner, width), BF16),
             pltpu.VMEM((2, inner, width), BF16),
             pltpu.VMEM((enc_taps, inner, inner), BF16),
@@ -708,12 +704,13 @@
             narrow(F32), narrow(F32), factor,
             wide(BF16),
             pltpu.VMEM((2, half, plan.ext, inner), BF16),
-            pltpu.VMEM((2, enc_taps, tokens, inner), BF16),
+            pltpu.VMEM((enc_taps + dec_taps, half, length, inner), BF16),
             narrow(BF16),
             wide(BF16),
             pltpu.VMEM((2, half, plan.ext, inner), BF16),
             narrow(BF16),
             wide(BF16),
+            pltpu.VMEM((1, half, length, inner), F32),
             pltpu.VMEM((plan.pool_rows, 128), BF16),
             pltpu.VMEM((plan.pool_rows, 128), BF16),
             pltpu.VMEM((plan.recv_rows, 128), BF16),

time: 103 us -> 96.3 us (0.935)
  Pallas kernels: 102 us -> 95.3 us
    pallas_call x1, Pallas kernels: 94.2 us -> 87.4 us  [per_device(): pl.pallas_call(functools.partial(main_kernel, plan), out_shape=(jax.Shape...]
where the time goes in v3:
time: 96.3 us; the launch traced here: 96.1 us
  Pallas kernels  95.3 us (99%)
    pallas_call x1, Pallas kernels, per_device(): pl.pallas_call(functools.partial(main_kernel, plan), out_shape=(jax.Shape...  87.4 us
    pallas_call x1, Pallas kernels, per_device(): pl.pallas_call(functools.partial(final_kernel, plan), out_shape=(jax.Shap...  7.94 us

profile of v3, /device:TPU:0, one launch (start us, length us, event | category | flops | bytes accessed | tf_op | source)
XLA Modules:
  0.0 96.1 jit_solution(12221465722012415625)
XLA Ops:
  0.7 87.4 %blocks_and_sums.1 = (bf16[1,4,192,800]{3,2,1,0:T(8,128)(2,1)}, bf16[1,4,192,800]{3,2,1,0:T(8,128)(2,1)}, bf16[20480,128]{1,0:T(8,128)(2,1)}, f32[16,512]{1,0:T(8,128)}) custom-call(bf16[1,4,192,800]{3,2,1,0:T(8,128)(2,1)} %refs_0_.1, bf16[4,192,800]{2,1,0:T(8,128)(2,1)} %refs_1_.1, s32[4,192]{1,0:T(4,128)} %refs_2_.1, f32[1,800]{1,0:T(1,128)} %refs_3_.1, ...), custom_call_target="tpu_custom_call" | custom-call | tf_op jit(solution)/shard_map/blocks_and_sums/pallas_call | solution.py:681
  88.0 7.9 %unpack_sums.1 = (bf16[1,4,192,800]{3,2,1,0:T(8,128)(2,1)}, bf16[1,4,192,800]{3,2,1,0:T(8,128)(2,1)}, f32[1,800]{1,0:T(1,128)}, f32[1,800]{1,0:T(1,128)}, f32[1,...) custom-call(bf16[1,4,192,800]{3,2,1,0:T(8,128)(2,1)} %get-tuple-elem, ...), custom_call_target="tpu_custom_call" | custom-call | tf_op jit(solution)/shard_map/unpack_sums/pallas_call | solution.py:733

commit v4 on v3

--- a/solution.py
+++ b/solution.py
@@ -68,7 +68,7 @@
 
 
 PARTS = 40
-CHUNKS = ((7, 'std'), (11, 'std'), (17, 'std'), (24, 'std'), (26, 'std'), (32, 'std'), (34, 'std'), (40, 'std'))
+CHUNKS = ((4, "std"), (11, "std"), (17, "std"), (19, "std"), (23, "std"), (29, "std"), (34, "std"), (38, "std"), (40, "std"))
 
 
 class Plan:
@@ -86,6 +86,7 @@
         self.up_rows = self.up_main * inner + self.up_rest * self.in_tiles
         self.down_rows = self.up_rows
         self.tap_rows = self.in_main * inner + self.in_rest * self.in_tiles
+        self.tap_part = self.tap_rows - inner // 2 // 128 * inner
         position = 0
         self.at = {}
         for name, block, size, pieces in (
@@ -137,7 +138,7 @@
         blocks_out, grads_out, pool_out, vec_out,
         xin, cot, wd, wu, ek, dk, vec, seg_side, masks,
         n1, s1, q1, n2, s2, q2, n3, s3, q3, fa, mid, win, la, outv, cp, hp, gin, dl,
-        pool, summed, recv, vsum, vtotal, vrecv,
+        pool, summed, recv, vsum, vtotal, vrecv, halo_bytes,
         load_sem, pair_send, pair_recv, seg_send, seg_recv, halo_send, halo_recv,
         pool_send, rs_recv, ag_recv, vec_send, vec_recv, out_sem, out_send, out_recv,
     ) = refs
@@ -158,7 +159,6 @@
         )
 
     own_rows = pl.ds(sec * half, half)
-    other_rows = pl.ds(other * half, half)
     loads = [
         pltpu.make_async_copy(blocks_in.at[0, own_rows], xin.at[sec], load_sem.at[0]),
         pltpu.make_async_copy(down_in.at[0], wd.at[sec], load_sem.at[1]),
@@ -167,14 +167,13 @@
         pltpu.make_async_copy(dec_in, dk, load_sem.at[4]),
         pltpu.make_async_copy(cot_in.at[own_rows], cot.at[0], load_sem.at[5]),
     ]
-    for load in loads:
-        load.start()
+    loads[0].start()
+    loads[1].start()
     vec[...] = jnp.zeros_like(vec)
     for at, ref in enumerate((in_gain, in_shift, up_bias)):
         vec[sec, at : at + 1, :] = ref[...]
     for at, ref in enumerate((down_bias, mid_gain, mid_shift, conv_bias, out_gain, out_shift)):
         vec[sec, 3 + at : 4 + at, :inner] = ref[...]
-    vsum[...] = jnp.zeros_like(vsum)
 
     known = {}
 
@@ -197,19 +196,31 @@
         pl.semaphore_signal(barrier, inc=1, device_id=peer, device_id_type=MESH)
     pl.semaphore_wait(barrier, len(greeted))
 
-    pair = [
-        remote(blocks_in.at[0, other_rows], xin.at[sec], pair_send.at[0], pair_recv.at[0], other_core),
-        remote(vec.at[sec], vec.at[sec], pair_send.at[1], pair_recv.at[1], other_core),
-        remote(down_in.at[0], wd.at[sec], pair_send.at[2], pair_recv.at[2], other_core),
-        remote(up_in.at[0], wu.at[sec], pair_send.at[3], pair_recv.at[3], other_core),
+    def pair(src, dst, at):
+        copy = remote(src, dst, pair_send.at[at], pair_recv.at[at], other_core)
+        copy.start()
+        return copy
+
+    def pair_rows(at, low, size):
+        for row in range(half):
+            rows = pl.ds(low, size)
+            pair(blocks_in.at[0, other * half + row, rows], xin.at[sec, row, rows], at)
+
+    pair(vec.at[sec], vec.at[sec], 0)
+    pair_rows(1, 0, MARGIN)
+    pair_rows(1, length - MARGIN, MARGIN)
+    pair(down_in.at[0], wd.at[sec], 2)
+    pair_rows(3, MARGIN, length - 2 * MARGIN)
+    pair(up_in.at[0], wu.at[sec], 4)
+    pair_whole = (
+        vec.at[other], xin.at[other, :, pl.ds(0, 2 * MARGIN)], wd.at[other],
+        xin.at[other, :, pl.ds(0, length - 2 * MARGIN)], wu.at[other],
+    )
+    arriving = [
+        remote(ref, ref, pair_send.at[at], pair_recv.at[at], other_core)
+        for at, ref in enumerate(pair_whole)
     ]
-    arriving = [
-        remote(ref.at[other], ref.at[other], pair_send.at[at], pair_recv.at[at], other_core)
-        for at, ref in enumerate((xin, vec, wd, wu))
-    ]
-    for copy in pair:
-        copy.start()
-    later_sends.extend(pair)
+    later_sends.extend(arriving)
     seg_copies = [
         remote(seg_in, seg_side.at[0], seg_send.at[0], seg_recv.at[0], right),
         remote(seg_in, seg_side.at[1], seg_send.at[1], seg_recv.at[1], left),
@@ -217,17 +228,20 @@
     for copy in seg_copies:
         copy.start()
     later_sends.extend(seg_copies)
-
-    def wait_block(block):
+    for load in loads[2:]:
+        load.start()
+    vsum[...] = jnp.zeros_like(vsum)
+
+    def wait_pair(block, local, away):
         @pl.when(sec == block)
         def _():
-            for load in loads[:3]:
-                load.wait()
+            for at in local:
+                loads[at].wait()
 
         @pl.when(sec != block)
         def _():
-            for copy in arriving:
-                copy.wait_recv()
+            for at in away:
+                arriving[at].wait_recv()
 
     def build_masks():
         for copy in seg_copies:
@@ -275,21 +289,26 @@
         narrow = [vec[block, 3 + at : 4 + at, :inner] for at in range(6)]
         return wide + narrow
 
-    def halo(ref, which, block):
-        copies = []
+    def halo_start(ref, which, block):
+        sems = halo_send.at[which, block], halo_recv.at[which, block]
         for row in range(half):
             if block == 0 or which == 0:
-                copies.append(remote(
+                remote(
                     ref.at[block, row, pl.ds(length, MARGIN)], ref.at[block, row, pl.ds(0, MARGIN)],
-                    halo_send.at[which, block, row, 0], halo_recv.at[which, block, row, 0], right,
-                ))
+                    *sems, right,
+                ).start()
             if block == 0 or which == 1:
-                copies.append(remote(
+                remote(
                     ref.at[block, row, pl.ds(MARGIN, MARGIN)],
-                    ref.at[block, row, pl.ds(length + MARGIN, MARGIN)],
-                    halo_send.at[which, block, row, 1], halo_recv.at[which, block, row, 1], left,
-                ))
-        return copies
+                    ref.at[block, row, pl.ds(length + MARGIN, MARGIN)], *sems, left,
+                ).start()
+
+    def halo_wait(which, block):
+        count = half * (2 if block == 0 else 1)
+        everything = halo_bytes.at[pl.ds(0, count)]
+        remote(
+            everything, everything, halo_send.at[which, block], halo_recv.at[which, block], right
+        ).wait()
 
     def entry(block, part):
         values = take(xin, block, part).astype(F32)
@@ -303,6 +322,8 @@
     def forward_in(block):
         p = params(block)
         for part in (edges, middle):
+            if part is middle:
+                wait_pair(block, (), (3,))
             normed, factor, act, slope = norm_act(entry(block, part), p[0], p[1])
             put(n1, block, part, normed)
             put(s1, block, part, slope)
@@ -316,13 +337,11 @@
             put(q2, block, part, spread(factor))
             put(mid, block, part, act.astype(BF16), MARGIN)
             if part is edges:
-                for copy in halo(mid, 0, block):
-                    copy.start()
+                halo_start(mid, 0, block)
 
     def forward_out(block):
         p = params(block)
-        for copy in halo(mid, 0, block):
-            copy.wait()
+        halo_wait(0, block)
         total = None
         for tap in range(plan.taps[block]):
             piece = window(mid, block, (tap - 2) * DILATION)
@@ -349,9 +368,11 @@
         return take(cot, 0, part) if block == 1 else take(gin, 1, part)
 
     def last_grad(block):
-        incoming = upstream_of(block, everywhere)
-        add_wide(block, 4, jnp.sum(incoming.astype(F32), axis=0, keepdims=True))
-        put(dl, 0, everywhere, dot(incoming, wu[block], 1, 1))
+        put(dl, 0, everywhere, dot(upstream_of(block, everywhere), wu[block], 1, 1))
+
+    def bias_sum(block):
+        incoming = upstream_of(block, everywhere).astype(F32)
+        add_wide(block, 4, jnp.sum(incoming, axis=0, keepdims=True))
 
     def backward_out(block):
         p = params(block)
@@ -371,13 +392,11 @@
             add_narrow(block, 9, jnp.sum(d_conv, axis=0, keepdims=True))
             put(cp, block, part, d_conv.astype(BF16), MARGIN)
             if part is edges:
-                for copy in halo(cp, 1, block):
-                    copy.start()
+                halo_start(cp, 1, block)
 
     def backward_mid(block):
         p = params(block)
-        for copy in halo(cp, 1, block):
-            copy.wait()
+        halo_wait(1, block)
         total = None
         for tap in range(plan.taps[block]):
             term = dot(window(cp, block, -(tap - 2) * DILATION), kernels[block][tap], 1, 1)
@@ -431,7 +450,7 @@
     def down_weight_grad(block):
         to_pool(plan.at["down", block], take(hp, block, everywhere), take(fa, block, everywhere))
 
-    pool_copies, running = [], {}
+    running = {}
 
     def sum_chunk(chunk):
         first, last, stages = plan.chunks[chunk]
@@ -483,9 +502,7 @@
             arriving = summed.at[pl.ds(first, (radix - 1) * size)]
             remote(arriving, arriving, pool_send.at[1], sem, others[0]).wait_recv()
         whole = pl.ds(first, last - first)
-        copy = pltpu.make_async_copy(summed.at[whole], pool_out.at[whole], out_sem.at[chunk])
-        copy.start()
-        pool_copies.append(copy)
+        pltpu.make_async_copy(summed.at[whole], pool_out.at[whole], out_sem.at[0]).start()
 
     def sum_vectors():
         total, slot = None, 0
@@ -524,34 +541,41 @@
 
     def send_result(at):
         value, result = ((outv, blocks_out), (gin, grads_out))[at]
-        for row in range(half):
-            target = result.at[0, sec * half + row]
-            landing = result.at[0, other * half + row]
-            local = pltpu.make_async_copy(value.at[sec, row], target, out_send.at[0, at, row])
-            sems = out_send.at[1, at, row], out_recv.at[at, row]
-            away = remote(value.at[other, row], target, *sems, other_core)
-            local.start()
-            away.start()
-            results.append((local, away, remote(value.at[other, row], landing, *sems, other_core)))
-
-    wait_block(0)
+        here, there = pl.ds(sec * half, half), pl.ds(other * half, half)
+        local = pltpu.make_async_copy(value.at[sec], result.at[0, here], out_send.at[0, at])
+        sems = out_send.at[1, at], out_recv.at[at]
+        away = remote(value.at[other], result.at[0, here], *sems, other_core)
+        local.start()
+        away.start()
+        results.append((local, away, remote(value.at[other], result.at[0, there], *sems, other_core)))
+
+    wait_pair(0, (0, 1), (0, 1, 2))
     forward_in(0)
     build_masks()
+    loads[5].wait()
+    bias_sum(1)
     loads[3].wait()
+    wait_pair(0, (2,), (4,))
     forward_out(0)
-    wait_block(1)
+    wait_pair(1, (0, 1), (0, 1, 2))
     forward_in(1)
-    loads[5].wait()
+    wait_pair(1, (2,), (4,))
     last_grad(1)
     loads[4].wait()
     forward_out(1)
-    send_result(0)
     if plan.pool_rows > plan.used_rows:
         pool[plan.used_rows : plan.pool_rows, :] = jnp.zeros(
             (plan.pool_rows - plan.used_rows, 128), BF16
         )
     run((
-        (backward_out, 1), (up_weight_grad, 1), (kernel_grad, 1, 0), 0, (backward_mid, 1), (kernel_grad, 1, 2), 0, (down_weight_grad, 1), (kernel_grad, 1, 1), 2, (backward_in, 1), 2, (backward_out, 0), 0, 1, (kernel_grad, 0, 0), (up_weight_grad, 0), (kernel_grad, 0, 1), 3, 1, (kernel_grad, 0, 2), (kernel_grad, 0, 3), 2, 5, 0, 3, (backward_mid, 0), 2, 1, 5, (down_weight_grad, 0), 0, (kernel_grad, 0, 4), 7, 3, 1, 7, 2, 5, 3, 0, 6, 4, 6, 1, 7, 4, 5, 0, 2, 3, 1, 7, 6, 4, 2, 5, 3, 4, 6, 7, 1, 5, 3, 4, 6, 2, 7, 0, 2, 1, 5, 6, 4, 0, 1, 7, 3, 4, 5, 6, (backward_in, 0), (send_result, 1), VECTORS, 7, 4, 6, 5, 3, 7, 4, 6,
+        (backward_out, 1), (up_weight_grad, 1), 0, (kernel_grad, 1, 2), (kernel_grad, 1, 0),
+        (kernel_grad, 1, 1), 0, 1, (backward_mid, 1), 1, (down_weight_grad, 1), 0, 2,
+        (backward_in, 1), 2, (up_weight_grad, 0), (backward_out, 0), 1, (kernel_grad, 0, 2), 0,
+        (kernel_grad, 0, 0), 4, (kernel_grad, 0, 1), 2, 5, (kernel_grad, 0, 4), 3, 4, 1,
+        (kernel_grad, 0, 3), 6, 3, 5, 2, 6, 0, (backward_mid, 0), 1, 4, 5, (down_weight_grad, 0),
+        (send_result, 0), (backward_in, 0), (send_result, 1), VECTORS, 8, 7, 3, 2, 6, 0, 7, 4, 8, 5,
+        1, 0, 6, 7, 2, 4, 3, 1, 5, 0, 7, VECTORS, 8, 2, 4, 6, 8, 3, 5, 4, 7, 6, 5, 8, VECTORS, 3, 4,
+        1, 2, 7, 4, 6, 8, 5, 2, VECTORS, 3, 7, 8, 0, 6, 3, 6, 1, 7, 3, 5, 8, 7, 8,
     ))
 
     while any(events is not None for events in running.values()):
@@ -561,8 +585,7 @@
         local.wait()
         away.wait_send()
         arrives.wait_recv()
-    for copy in pool_copies:
-        copy.wait()
+    pltpu.make_async_copy(summed, pool_out, out_sem.at[0]).wait()
     for copy in later_sends:
         copy.wait_send()
     for at in range(2):
@@ -571,12 +594,12 @@
     remote(vrecv, vrecv, vec_send.at[0], vec_recv.at[0], other_core).wait_send()
 
 
-def final_kernel(plan, blocks_in, grads_in, pool_in, vec, *refs):
+def final_kernel(plan, blocks_in, grads_in, pool_in, vec_in, *refs):
     (
         blocks_out, grads_out, g_in_gain, g_in_shift, g_down, g_down_bias, g_mid_gain, g_mid_shift,
         g_enc, g_dec, g_conv_bias, g_out_gain, g_out_shift, g_up, g_up_bias,
-        bounce, up_pool, down_pool, tap_pool, up_full, down_full, enc_full, dec_full,
-        in_sem, out_sem,
+        vec, wide_out, narrow_out, bounce, up_pool, down_pool, tap_pool, up_full, down_full, enc_full, dec_full,
+        in_sem, out_sem, vec_sem,
     ) = refs
     sec = lax.axis_index("section")
     width, inner = plan.width, plan.inner
@@ -584,6 +607,8 @@
         pltpu.make_async_copy(blocks_in, bounce.at[0], in_sem.at[4]),
         pltpu.make_async_copy(grads_in, bounce.at[1], in_sem.at[5]),
     ]
+    vec_load = pltpu.make_async_copy(vec_in, vec, vec_sem.at[0])
+    vec_load.start()
     passed = [
         pltpu.make_async_copy(bounce.at[0], blocks_out, out_sem.at[0]),
         pltpu.make_async_copy(bounce.at[1], grads_out, out_sem.at[1]),
@@ -600,23 +625,31 @@
     up_load = load("up", up_pool, plan.up_rows, 0)
     down_load = load("down", down_pool, plan.down_rows, 1)
     tap_loads = []
-    at = 0
+    part = inner // 2
+    low = part // 128
+    lanes = (plan.in_tiles - 1 - low) * 128
+    size = plan.tap_part
+    first_tile = sec * low
     for block in (0, 1):
-        size = plan.tap_rows * plan.taps[block]
-        start = plan.at["kernel", block]
-        copy = pltpu.make_async_copy(pool_in.at[pl.ds(start, size)], tap_pool.at[pl.ds(at, size)], in_sem.at[2 + block])
-        copy.start()
-        tap_loads.append(copy)
-        at += size
-
-    def wide(at):
-        return jnp.concatenate([vec[at : at + 1, :], vec[at + 1 : at + 2, : width - 512]], axis=1)
-
-    g_in_gain[...] = wide(0)
-    g_in_shift[...] = wide(2)
-    g_up_bias[...] = wide(4)
+        for tap in range(plan.taps[block]):
+            start = plan.at["kernel", block] + tap * plan.tap_rows + first_tile * inner
+            at = len(tap_loads)
+            copy = pltpu.make_async_copy(
+                pool_in.at[pl.ds(pl.multiple_of(start, 16), size)], tap_pool.at[at], in_sem.at[6 + at]
+            )
+            copy.start()
+            tap_loads.append(copy)
+
+    vec_load.wait()
+    for at, ref in enumerate((g_in_gain, g_in_shift, g_up_bias)):
+        pieces = [vec[2 * at : 2 * at + 1, :], vec[2 * at + 1 : 2 * at + 2, : width - 512]]
+        wide_out[at] = jnp.concatenate(pieces, axis=1)
+        passed.append(pltpu.make_async_copy(wide_out.at[at], ref, vec_sem.at[1 + at]))
+        passed[-1].start()
     for at, ref in enumerate((g_down_bias, g_mid_gain, g_mid_shift, g_conv_bias, g_out_gain, g_out_shift)):
-        ref[...] = vec[6 + at : 7 + at, :inner]
+        narrow_out[at] = vec[6 + at : 7 + at, :inner]
+        passed.append(pltpu.make_async_copy(narrow_out.at[at], ref, vec_sem.at[4 + at]))
+        passed[-1].start()
 
     def rest_of(ref, position, rest, tiles):
         pieces = [ref[position + tile * rest : position + (tile + 1) * rest, :] for tile in range(tiles)]
@@ -639,26 +672,24 @@
     unpack(down_pool, down_full, inner, plan.up_main, plan.up_rest, plan.in_tiles)
     down_store = pltpu.make_async_copy(down_full, g_down.at[0], out_sem.at[3])
     down_store.start()
-    part = inner // 2
-    row = lax.broadcasted_iota(jnp.int32, (inner, part), 0)
-    column = lax.broadcasted_iota(jnp.int32, (inner, part), 1)
-    choose = jnp.where(row == column + sec * part, 1.0, 0.0).astype(BF16)
+    taken = lanes + plan.in_rest
+    row = lax.broadcasted_iota(jnp.int32, (taken, part), 0)
+    column = lax.broadcasted_iota(jnp.int32, (taken, part), 1)
+    choose = jnp.where(row == column + sec * (part - low * 128), 1.0, 0.0).astype(BF16)
     stores = []
-    at = 0
     for block, full, target in ((0, enc_full, g_enc), (1, dec_full, g_dec)):
-        tap_loads[block].wait()
         for tap in range(plan.taps[block]):
+            at = tap + block * plan.taps[0]
+            tap_loads[at].wait()
             main = jnp.concatenate(
-                [tap_pool[at + tile * inner : at + (tile + 1) * inner, :] for tile in range(plan.in_main)], axis=1
+                [tap_pool[at, tile * inner : (tile + 1) * inner, :] for tile in range(lanes // 128)], axis=1
             )
-            lanes = plan.in_main * 128
-            rest = rest_of(tap_pool, at + plan.in_main * inner, plan.in_rest, plan.in_tiles)
+            rest = rest_of(tap_pool.at[at], lanes // 128 * inner, plan.in_rest, plan.in_tiles)
             rest = rest[:, :inner].astype(BF16)
             full[tap] = dot(main, choose[:lanes], 1, 0) + dot(rest, choose[lanes:], 0, 0)
-            at += plan.tap_rows
-        copy = pltpu.make_async_copy(full, target, out_sem.at[4 + block])
-        copy.start()
-        stores.append(copy)
+            copy = pltpu.make_async_copy(full.at[tap], target.at[tap], out_sem.at[4 + at])
+            copy.start()
+            stores.append(copy)
     for copy in passed + [up_store, down_store] + stores:
         copy.wait()
 
@@ -717,11 +748,11 @@
             pltpu.VMEM((2, 16, 512), F32),
             pltpu.VMEM((len(plan.vec_stages), 16, 512), F32),
             pltpu.VMEM((plan.vec_copies, 16, 512), F32),
-            dma((6,)), dma((4,)), dma((4,)), dma((2,)), dma((2,)),
-            dma((2, 2, half, 2)), dma((2, 2, half, 2)),
+            pltpu.VMEM((2 * half, MARGIN, inner), BF16),
+            dma((6,)), dma((5,)), dma((5,)), dma((2,)), dma((2,)), dma((2, 2)), dma((2, 2)),
             dma((2,)), dma((chunks * plan.most_stages,)), dma((chunks * plan.most_stages,)),
             dma((1,)), dma((len(plan.vec_stages),)),
-            dma((chunks,)), dma((2, 2, half)), dma((2, half)),
+            dma((1,)), dma((2, 2)), dma((2,)),
         ],
         compiler_params=pltpu.CompilerParams(
             collective_id=0, has_side_effects=True, vmem_limit_bytes=VMEM_LIMIT
@@ -744,19 +775,21 @@
             jax.ShapeDtypeStruct((1, inner, width), F32),
             vector(width),
         ),
-        in_specs=[any_spec, any_spec, any_spec, vmem_spec],
-        out_specs=(any_spec, any_spec, vmem_spec, vmem_spec, any_spec, vmem_spec, vmem_spec, vmem_spec,
-                   any_spec, any_spec, vmem_spec, vmem_spec, vmem_spec, any_spec, vmem_spec),
+        in_specs=[any_spec] * 4,
+        out_specs=(any_spec,) * 15,
         scratch_shapes=[
+            pltpu.VMEM((16, 512), F32),
+            pltpu.VMEM((3, 1, width), F32),
+            pltpu.VMEM((6, 1, inner), F32),
             pltpu.VMEM((2,) + block_inputs.shape, BF16),
             pltpu.VMEM((plan.up_rows, 128), BF16),
             pltpu.VMEM((plan.down_rows, 128), BF16),
-            pltpu.VMEM((plan.tap_rows * (enc_taps + dec_taps), 128), BF16),
+            pltpu.VMEM((enc_taps + dec_taps, plan.tap_part, 128), BF16),
             pltpu.VMEM((inner, width), F32),
             pltpu.VMEM((inner, width), F32),
             pltpu.VMEM((enc_taps, inner, part), F32),
             pltpu.VMEM((dec_taps, inner, part), F32),
-            dma((6,)), dma((6,)),
+            dma((6 + enc_taps + dec_taps,)), dma((4 + enc_taps + dec_taps,)), dma((10,)),
         ],
         compiler_params=pltpu.CompilerParams(vmem_limit_bytes=VMEM_LIMIT),
         name="unpack_sums",

time: 96.3 us -> 87.4 us (0.908)
  Pallas kernels: 95.3 us -> 86.4 us
    pallas_call x1, Pallas kernels: 87.4 us -> 79.6 us  [per_device(): pl.pallas_call(functools.partial(main_kernel, plan), out_shape=(jax.Shape...]
    pallas_call x1, Pallas kernels: 7.94 us -> 6.82 us  [per_device(): pl.pallas_call(functools.partial(final_kernel, plan), out_shape=(jax.Shap...]
where the time goes in v4:
time: 87.4 us; the launch traced here: 87.2 us
  Pallas kernels  86.4 us (99%)
    pallas_call x1, Pallas kernels, per_device(): pl.pallas_call(functools.partial(main_kernel, plan), out_shape=(jax.Shape...  79.6 us
    pallas_call x1, Pallas kernels, per_device(): pl.pallas_call(functools.partial(final_kernel, plan), out_shape=(jax.Shap...  6.82 us

profile of v4, /device:TPU:0, one launch (start us, length us, event | category | flops | bytes accessed | tf_op | source)
XLA Modules:
  0.0 87.2 jit_solution(17327669407790919416)
XLA Ops:
  0.7 79.6 %blocks_and_sums.1 = (bf16[1,4,192,800]{3,2,1,0:T(8,128)(2,1)}, bf16[1,4,192,800]{3,2,1,0:T(8,128)(2,1)}, bf16[20480,128]{1,0:T(8,128)(2,1)}, f32[16,512]{1,0:T(8,128)}) custom-call(bf16[1,4,192,800]{3,2,1,0:T(8,128)(2,1)} %refs_0_.1, bf16[4,192,800]{2,1,0:T(8,128)(2,1)} %refs_1_.1, s32[4,192]{1,0:T(4,128)} %refs_2_.1, f32[1,800]{1,0:T(1,128)} %refs_3_.1, ...), custom_call_target="tpu_custom_call" | custom-call | tf_op jit(solution)/shard_map/blocks_and_sums/pallas_call | solution.py:712
  80.2 6.8 %unpack_sums.1 = (bf16[1,4,192,800]{3,2,1,0:T(8,128)(2,1)}, bf16[1,4,192,800]{3,2,1,0:T(8,128)(2,1)}, f32[1,800]{1,0:T(1,128)}, f32[1,800]{1,0:T(1,128)}, f32[1,...) custom-call(bf16[1,4,192,800]{3,2,1,0:T(8,128)(2,1)} %get-tuple-elem, ...), custom_call_target="tpu_custom_call" | custom-call | tf_op jit(solution)/shard_map/unpack_sums/pallas_call | solution.py:764

commit v5 on v4

--- a/solution.py
+++ b/solution.py
@@ -68,7 +68,7 @@
 
 
 PARTS = 40
-CHUNKS = ((4, "std"), (11, "std"), (17, "std"), (19, "std"), (23, "std"), (29, "std"), (34, "std"), (38, "std"), (40, "std"))
+CHUNKS = ((4, "std"), (11, "std"), (17, "std"), (22, "std"), (24, "std"), (28, "std"), (32, "std"), (35, "std"), (38, "std"), (40, "std"))
 
 
 class Plan:
@@ -568,14 +568,15 @@
             (plan.pool_rows - plan.used_rows, 128), BF16
         )
     run((
-        (backward_out, 1), (up_weight_grad, 1), 0, (kernel_grad, 1, 2), (kernel_grad, 1, 0),
-        (kernel_grad, 1, 1), 0, 1, (backward_mid, 1), 1, (down_weight_grad, 1), 0, 2,
-        (backward_in, 1), 2, (up_weight_grad, 0), (backward_out, 0), 1, (kernel_grad, 0, 2), 0,
-        (kernel_grad, 0, 0), 4, (kernel_grad, 0, 1), 2, 5, (kernel_grad, 0, 4), 3, 4, 1,
-        (kernel_grad, 0, 3), 6, 3, 5, 2, 6, 0, (backward_mid, 0), 1, 4, 5, (down_weight_grad, 0),
-        (send_result, 0), (backward_in, 0), (send_result, 1), VECTORS, 8, 7, 3, 2, 6, 0, 7, 4, 8, 5,
-        1, 0, 6, 7, 2, 4, 3, 1, 5, 0, 7, VECTORS, 8, 2, 4, 6, 8, 3, 5, 4, 7, 6, 5, 8, VECTORS, 3, 4,
-        1, 2, 7, 4, 6, 8, 5, 2, VECTORS, 3, 7, 8, 0, 6, 3, 6, 1, 7, 3, 5, 8, 7, 8,
+        (up_weight_grad, 1), 0, (backward_out, 1), (kernel_grad, 1, 0), (kernel_grad, 1, 2),
+        (kernel_grad, 1, 1), 0, 1, (backward_mid, 1), 1, (down_weight_grad, 1), 2, (backward_in, 1),
+        0, 2, (backward_out, 0), (up_weight_grad, 0), 1, 3, (kernel_grad, 0, 0),
+        (kernel_grad, 0, 2), 0, (kernel_grad, 0, 1), 4, 3, 5, 2, (kernel_grad, 0, 3), 4, 1, 6, 5,
+        (backward_mid, 0), (send_result, 0), 0, 2, 3, (kernel_grad, 0, 4), 6, (down_weight_grad, 0),
+        8, 9, 5, 1, 7, 4, 8, 3, 9, 7, 0, (backward_in, 0), (send_result, 1), 2, 6, VECTORS, 8,
+        VECTORS, 5, 4, 1, 3, 7, 9, 0, 8, 6, 2, 1, 4, 5, 3, 7, 9, 8, 2, 6, 4, 5, 3, 7, 9, 8, 4,
+        VECTORS, 6, 0, 5, 7, 2, 9, 0, 8, 1, 6, 7, 9, VECTORS, 2, 5, 3, 8, 5, 4, 8, 1, 6, 7, 4, 9, 6,
+        3, 7, 9,
     ))
 
     while any(events is not None for events in running.values()):

time: 87.4 us -> 86.1 us (0.985)
  Pallas kernels: 86.4 us -> 85 us
    pallas_call x1, Pallas kernels: 79.6 us -> 78.2 us  [per_device(): pl.pallas_call(functools.partial(main_kernel, plan), out_shape=(jax.Shape...]
where the time goes in v5:
time: 86.1 us; the launch traced here: 85.9 us
  Pallas kernels  85 us (99%)
    pallas_call x1, Pallas kernels, per_device(): pl.pallas_call(functools.partial(main_kernel, plan), out_shape=(jax.Shape...  78.2 us
    pallas_call x1, Pallas kernels, per_device(): pl.pallas_call(functools.partial(final_kernel, plan), out_shape=(jax.Shap...  6.82 us

profile of v5, /device:TPU:0, one launch (start us, length us, event | category | flops | bytes accessed | tf_op | source)
XLA Modules:
  0.0 85.9 jit_solution(2686895975602549276)
XLA Ops:
  0.7 78.2 %blocks_and_sums.1 = (bf16[1,4,192,800]{3,2,1,0:T(8,128)(2,1)}, bf16[1,4,192,800]{3,2,1,0:T(8,128)(2,1)}, bf16[20480,128]{1,0:T(8,128)(2,1)}, f32[16,512]{1,0:T(8,128)}) custom-call(bf16[1,4,192,800]{3,2,1,0:T(8,128)(2,1)} %refs_0_.1, bf16[4,192,800]{2,1,0:T(8,128)(2,1)} %refs_1_.1, s32[4,192]{1,0:T(4,128)} %refs_2_.1, f32[1,800]{1,0:T(1,128)} %refs_3_.1, ...), custom_call_target="tpu_custom_call" | custom-call | tf_op jit(solution)/shard_map/blocks_and_sums/pallas_call | solution.py:713
  78.9 6.8 %unpack_sums.1 = (bf16[1,4,192,800]{3,2,1,0:T(8,128)(2,1)}, bf16[1,4,192,800]{3,2,1,0:T(8,128)(2,1)}, f32[1,800]{1,0:T(1,128)}, f32[1,800]{1,0:T(1,128)}, f32[1,...) custom-call(bf16[1,4,192,800]{3,2,1,0:T(8,128)(2,1)} %get-tuple-elem, ...), custom_call_target="tpu_custom_call" | custom-call | tf_op jit(solution)/shard_map/unpack_sums/pallas_call | solution.py:765
